TPU v7x, 512 devices: a whole 4x4x16 slice. The times are simulated.
512 devices in a mesh: tm: 8 (over x, y_lo), height: 64 (over z, y_hi, core).
Axes of the slice: x: 4, y: 4 (y_hi: 2, y_lo: 2; y = y_hi * 2 + y_lo), z: 16, core: 2. Of those that a mesh axis runs over, the one named last changes fastest.
Arguments:
- query_raw: bfloat16 [16, 64, 80, 1536], P('tm', 'height'), may hold values from -40 to 40
- key_raw: bfloat16 [16, 64, 80, 1536], P('tm', 'height'), may hold values from -40 to 40
- values: bfloat16 [16, 64, 80, 1536], P('tm', 'height'), may hold values from -6 to 6
- out_grad: bfloat16 [16, 64, 80, 1536], P('tm', 'height'), may hold values from -6 to 6
- query_gain: float32 [128], replicated, may hold values from 0.5 to 1.5
- key_gain: float32 [128], replicated, may hold values from 0.5 to 1.5
- window: int32 [12, 3], replicated, may hold values from 0 to 2, as said below
Outputs:
- query_grad: bfloat16 [16, 64, 80, 1536], P('tm', 'height')
- key_grad: bfloat16 [16, 64, 80, 1536], P('tm', 'height')
- value_grad: bfloat16 [16, 64, 80, 1536], P('tm', 'height')
- gain_grad: float32 [2, 128], P(None, 'height')
Inputs may be any that keep to these rules, and one draw needn't show every extreme that they name: `window`: columns 0 and 1 hold 0 or 1 and column 2 holds 0 to 2; some head has reach (1, 1, 2) and some head (0, 0, 0).
All inputs are finite; a program needn't handle non-finite values.
Results may differ from a plain program's by a relative error of at most 0.008.
Values may be sent and summed in bfloat16 or wider, within the bound.
No kernel may reach another device: no remote copies, remote signals or barrier semaphores. Data moves between devices by JAX's collectives and lax.ppermute only.
A program may use at most 128 MiB of HBM per device.

v0:
```python
import math

import jax
import jax.numpy as jnp
from jax import lax
from jax.sharding import PartitionSpec as P

TILE_W = 8


EPSILON = 1e-06


def from_behind(block, axis, distance):
    devices = range(lax.axis_size(axis))
    route = [(i - distance, i) for i in devices if i - distance in devices]
    return lax.ppermute(block, axis, route)


def with_halo(x, sides, width):
    for axis, dim in sides:
        size, length = (lax.axis_size(axis), x.shape[dim])
        up = [(i, (i + 1) % size) for i in range(size - 1)]
        down = [(j, i) for i, j in up]
        last = lax.slice_in_dim(x, length - width, length, axis=dim)
        initial = lax.slice_in_dim(x, 0, width, axis=dim)
        before = lax.ppermute(last, axis, up)
        after = lax.ppermute(initial, axis, down)
        x = jnp.concatenate([before, x, after], axis=dim)
    return x


def normalize(raw_rows, gain_vector):
    full_rows = raw_rows.astype(jnp.float32)
    inverse = lax.rsqrt(jnp.mean(full_rows * full_rows, axis=-1, keepdims=True) + EPSILON)
    unit_rows = full_rows * inverse
    return ((unit_rows * gain_vector).astype(jnp.bfloat16), unit_rows, inverse)


def norm_backward(grad_rows, unit_rows, inverse, gain_vector):
    scaled = grad_rows * gain_vector
    return inverse * (scaled - unit_rows * jnp.mean(unit_rows * scaled, axis=-1, keepdims=True))


def positions(frame_start, row_start, frame_count, row_count, columns):
    frame_ids = frame_start + jnp.arange(frame_count, dtype=jnp.int32)
    row_ids = row_start + jnp.arange(row_count, dtype=jnp.int32)
    column_ids = jnp.arange(columns, dtype=jnp.int32)
    grid_shape = (frame_count, row_count, columns)
    frame_grid = jnp.broadcast_to(frame_ids[:, None, None], grid_shape).reshape(-1)
    row_grid = jnp.broadcast_to(row_ids[None, :, None], grid_shape).reshape(-1)
    column_grid = jnp.broadcast_to(column_ids[None, None, :], grid_shape).reshape(-1)
    return (frame_grid, row_grid, column_grid)


def gap_tables(query_pos, key_pos, query_valid, key_valid):
    frame_gap = jnp.abs(query_pos[0][:, None] - key_pos[0][None, :])
    row_gap = jnp.abs(query_pos[1][:, None] - key_pos[1][None, :])
    tile_gap = jnp.abs(query_pos[2][:, None] // TILE_W - key_pos[2][None, :] // TILE_W)
    inside = query_valid[:, None] & key_valid[None, :]
    return (frame_gap, row_gap, tile_gap, inside)


def allowed_for(tables, window_part):
    frame_gap, row_gap, tile_gap, inside = tables
    return (
        (frame_gap[None] <= window_part[:, 0, None, None])
        & (row_gap[None] <= window_part[:, 1, None, None])
        & (tile_gap[None] <= window_part[:, 2, None, None])
        & inside[None]
    )


def probabilities(queries, key_rows, allowed, row_total):
    score_scale = queries.shape[-1] ** (-0.5)
    scores = (
        jnp.einsum("qgd,kgd->gqk", queries, key_rows, preferred_element_type=jnp.float32)
        * score_scale
    )
    weight = jnp.where(allowed, jnp.exp(scores), 0.0)
    row_total = jnp.sum(weight, axis=-1)
    return (weight / row_total[..., None], row_total)


def score_grads(attention, prob_back, row_delta, head_dim):
    return (attention * (prob_back - row_delta[..., None]) * head_dim ** (-0.5)).astype(
        jnp.bfloat16
    )


def full_pass(queries, grad_rows, key_rows, value_rows, allowed):
    attention, row_total = probabilities(queries, key_rows, allowed, None)
    prob_back = jnp.einsum(
        "qgd,kgd->gqk", grad_rows, value_rows, preferred_element_type=jnp.float32
    )
    row_delta = jnp.sum(attention * prob_back, axis=-1)
    score_back = score_grads(attention, prob_back, row_delta, queries.shape[-1])
    query_back = jnp.einsum(
        "gqk,kgd->qgd", score_back, key_rows, preferred_element_type=jnp.float32
    )
    key_back = jnp.einsum("gqk,qgd->kgd", score_back, queries, preferred_element_type=jnp.float32)
    value_back = jnp.einsum(
        "gqk,qgd->kgd",
        attention.astype(jnp.bfloat16),
        grad_rows,
        preferred_element_type=jnp.float32,
    )
    return (query_back, key_back, value_back)


def send_rows(piece_rows, offset):
    return from_behind(piece_rows.astype(jnp.bfloat16), "height", offset).astype(piece_rows.dtype)


def send_frames(piece_rows, offset):
    return from_behind(piece_rows.astype(jnp.bfloat16), "tm", offset).astype(piece_rows.dtype)


def on_device(query_raw, key_raw, values, out_grad, query_gain, key_gain, window):
    frames_dev, rows_dev, columns, channels = query_raw.shape
    head_count = window.shape[0]
    head_dim = channels // head_count
    own_count = frames_dev * rows_dev * columns
    ext_frames = frames_dev + 2
    ext_rows = rows_dev + 2
    ext_count = ext_frames * ext_rows * columns
    frame_start = lax.axis_index("tm") * frames_dev
    row_start = lax.axis_index("height") * rows_dev
    all_frames = frames_dev * lax.axis_size("tm")
    all_rows = rows_dev * lax.axis_size("height")
    flat_shape = (own_count, head_count, head_dim)
    block_shape = (frames_dev, rows_dev, columns, channels)
    group_size = math.gcd(head_count, 4)
    head_starts = list(range(0, head_count, group_size))

    def head_slice(array_rows, head_first):
        return array_rows[:, head_first : head_first + group_size]

    query_norm, query_unit, query_inverse = normalize(query_raw.reshape(flat_shape), query_gain)
    key_norm, key_unit, key_inverse = normalize(key_raw.reshape(flat_shape), key_gain)
    grad_flat = out_grad.reshape(flat_shape)
    own_pos = positions(frame_start, row_start, frames_dev, rows_dev, columns)
    ext_pos = positions(frame_start - 1, row_start - 1, ext_frames, ext_rows, columns)
    ext_valid = (
        (ext_pos[0] >= 0) & (ext_pos[0] < all_frames) & (ext_pos[1] >= 0) & (ext_pos[1] < all_rows)
    )
    own_valid = jnp.ones((own_count,), jnp.bool_)
    paired = jnp.stack([key_norm.reshape(block_shape), values])
    extended = with_halo(paired, (("tm", 1), ("height", 2)), 1)
    ext_keys = extended[0].reshape(ext_count, head_count, head_dim)
    ext_values = extended[1].reshape(ext_count, head_count, head_dim)
    row_tables = gap_tables(own_pos, ext_pos, own_valid, ext_valid)
    pieces = [
        full_pass(
            head_slice(query_norm, head_first),
            head_slice(grad_flat, head_first),
            head_slice(ext_keys, head_first),
            head_slice(ext_values, head_first),
            allowed_for(row_tables, window[head_first : head_first + group_size]),
        )
        for head_first in head_starts
    ]
    query_back = jnp.concatenate([piece_rows[0] for piece_rows in pieces], axis=1)
    key_ext = jnp.concatenate([piece_rows[1] for piece_rows in pieces], axis=1)
    value_ext = jnp.concatenate([piece_rows[2] for piece_rows in pieces], axis=1)
    gathered = jnp.stack([key_ext, value_ext]).reshape(2, ext_frames, ext_rows, columns, channels)
    from_above = send_rows(gathered[:, :, :1], -1)
    from_below = send_rows(gathered[:, :, ext_rows - 1 :], 1)
    middle = gathered[:, :, 1 : ext_rows - 1]
    middle = middle.at[:, :, rows_dev - 1 : rows_dev].add(from_above)
    middle = middle.at[:, :, 0:1].add(from_below)
    from_next = send_frames(middle[:, :1], -1)
    from_prev = send_frames(middle[:, ext_frames - 1 :], 1)
    owned_rows = middle[:, 1 : ext_frames - 1]
    owned_rows = owned_rows.at[:, frames_dev - 1 : frames_dev].add(from_next)
    owned_rows = owned_rows.at[:, 0:1].add(from_prev)
    key_back = owned_rows[0].reshape(flat_shape)
    value_back = owned_rows[1].reshape(flat_shape)
    query_grad = (
        norm_backward(query_back, query_unit, query_inverse, query_gain)
        .astype(jnp.bfloat16)
        .reshape(block_shape)
    )
    key_grad = (
        norm_backward(key_back, key_unit, key_inverse, key_gain)
        .astype(jnp.bfloat16)
        .reshape(block_shape)
    )
    value_grad = value_back.astype(jnp.bfloat16).reshape(block_shape)
    gain_part = jnp.stack(
        [jnp.sum(query_back * query_unit, axis=(0, 1)), jnp.sum(key_back * key_unit, axis=(0, 1))]
    )
    owner_part = lax.psum_scatter(gain_part, "height", scatter_dimension=1, tiled=True)
    gain_grad = lax.psum(owner_part, "tm")
    return (query_grad, key_grad, value_grad, gain_grad)


def solution(mesh):
    return jax.shard_map(
        on_device,
        mesh=mesh,
        in_specs=(
            P("tm", "height", None, None),
            P("tm", "height", None, None),
            P("tm", "height", None, None),
            P("tm", "height", None, None),
            P(),
            P(),
            P(),
        ),
        out_specs=(
            P("tm", "height", None, None),
            P("tm", "height", None, None),
            P("tm", "height", None, None),
            P(None, "height"),
        ),
        check_vma=False,
    )
```

profile of v0, /device:TPU:8, one launch (start us, length us, event | category | flops | bytes accessed | tf_op | source)
XLA Modules:
  0.0 457.0 jit_solution(10019195043343687009)
XLA Ops:
  8.5 3.3 collective-permute-start
  11.8 6.6 %collective-permute-start.1 = (bf16[2,1,1,80,1536]{4,3,1,2,0:T(8,128)(2,1)}, bf16[2,1,1,80,1536]{4,3,1,2,0:T(8,128)(2,1)}, u32[]{:S(2)}, u32[]{:S(2)}) collective-permute-start(bf16[2,1,1,80,1536]{4,3,1,2,0:T(8,128)(2,1)} %get-tuple-element.113), channel_id=1, source_target_pairs={{64,0},{128,64},{192,128},{256,192},{320,256},{384,320},{448,384},... | collective-permute-start | bytes 1474568 | tf_op jit(solution)/shard_map/ppermute | solution.py:28
  23.2 11.0 %collective-permute-done = bf16[2,1,1,80,1536]{4,3,1,2,0:T(8,128)(2,1)} collective-permute-done((bf16[2,1,1,80,1536]{4,3,1,2,0:T(8,128)(2,1)}, bf16[2,1,1,80,1536]{4,3,1,2,0:T(8,128)(2,1)}, u32[]{:S(2)}, u32[]{:S(2)}) %collective-permute-start) | collective-permute-done | bytes 491552 | tf_op jit(solution)/shard_map/ppermute | solution.py:27
  34.2 2.9 pad_maximum_fusion.4
  38.6 4.5 collective-permute-start.2
  52.1 3.4 pad_maximum_fusion.1
  59.5 6.5 %reshape_squeeze.13 = bf16[960,12,128]{2,1,0:T(8,128)(2,1)} reshape(bf16[1,4,3,80,1536]{4,3,2,1,0:T(8,128)(2,1)} %copy.125) | data formatting | bytes 5898240 | tf_op jit(solution)/shard_map/reshape;squeeze | solution.py:151
  66.1 5.2 %fusion.78 = (bf16[960,4,128]{2,1,0:T(4,128)(2,1)}, bf16[960,4,128]{2,1,0:T(4,128)(2,1)}, bf16[960,4,128]{2,1,0:T(4,128)(2,1)}) fusion(bf16[960,12,128]{2,1,0:T(8,128)(2,1)} %reshape_squeeze.13), kind=kLoop, calls=%fused_computation.157 | loop fusion | bytes 5898240 | tf_op jit(solution)/shard_map/slice | solution.py:137
  73.0 6.5 %reshape_squeeze.12 = bf16[960,12,128]{2,1,0:T(8,128)(2,1)} reshape(bf16[1,4,3,80,1536]{4,3,2,1,0:T(8,128)(2,1)} %copy.122) | data formatting | bytes 5898240 | tf_op jit(solution)/shard_map/reshape;squeeze | solution.py:150
  79.6 5.1 %fusion.79 = (bf16[960,4,128]{2,1,0:T(4,128)(2,1)S(1)}, bf16[960,4,128]{2,1,0:T(4,128)(2,1)}, bf16[960,4,128]{2,1,0:T(4,128)(2,1)}) fusion(bf16[960,12,128]{2,1,0:T(8,128)(2,1)} %reshape_squeeze.12), kind=kLoop, calls=%fused_computation.158 | loop fusion | bytes 5898240 | tf_op jit(solution)/shard_map/slice | solution.py:137
  91.6 6.6 %convolution_bitcast_fusion.5 = f32[960,4,128]{2,0,1:T(8,128)} fusion(bf16[160,12,128]{2,0,1:T(8,128)(2,1)} %multiply_convert_fusion.1, f32[4,160,960]{2,1,0:T(8,128)} %copy-done.14, f32[4,960,160]{1,2,0:T(8,128)} %fusion.37), kind=kOutput, calls=%fused_computation.33 | convolution fusion | flops 160360000 | bytes 7372800 | tf_op jit(solution)/shard_map/gqk,qgd->kgd/dot_general | solution.py:101
  98.2 2.8 exponential_select_fusion.1
  106.3 6.6 %convolution_bitcast_fusion.4 = f32[960,4,128]{2,0,1:T(8,128)} fusion(bf16[160,12,128]{2,0,1:T(8,128)(2,1)S(1)} %copy-done.23, f32[4,160,960]{2,1,0:T(8,128)} %copy-done.15, f32[4,960,160]{1,2,0:T(8,128)} %fusion.35), kind=kOutput, calls=%fused_computation.32 | convolution fusion | flops 160360000 | bytes 7372800 | tf_op jit(solution)/shard_map/gqk,qgd->kgd/dot_general | solution.py:101
  112.9 2.8 exponential_select_fusion
  121.2 6.5 %convolution_bitcast_fusion.3 = f32[960,4,128]{2,0,1:T(8,128)} fusion(bf16[160,12,128]{2,0,1:T(8,128)(2,1)S(1)} %copy-done.23, f32[4,160,960]{2,1,0:T(8,128)} %copy-done.16, f32[4,960,160]{1,2,0:T(8,128)} %fusion.33), kind=kOutput, calls=%fused_computation.31 | convolution fusion | flops 160360000 | bytes 7372800 | tf_op jit(solution)/shard_map/gqk,qgd->kgd/dot_general | solution.py:101
  127.6 3.1 pad_maximum_fusion.2
  130.8 6.6 %copy.136 = f32[960,12,128]{2,1,0:T(8,128)} copy(f32[960,12,128]{2,0,1:T(8,128)S(1)} %pad_maximum_fusion.2) | data formatting | bytes 11796480 | tf_op jit(solution)/shard_map/concatenate | solution.py:164
  137.3 8.2 %stack.26 = f32[1,4,3,80,1536]{4,3,2,1,0:T(8,128)} reshape(f32[960,12,128]{2,1,0:T(8,128)} %copy.136) | data formatting | bytes 11796480 | tf_op jit(solution)/shard_map/stack | solution.py:166
  145.5 3.1 pad_maximum_fusion.3
  148.6 6.6 %copy.137 = f32[960,12,128]{2,1,0:T(8,128)} copy(f32[960,12,128]{2,0,1:T(8,128)S(1)} %pad_maximum_fusion.3) | data formatting | bytes 11796480 | tf_op jit(solution)/shard_map/concatenate | solution.py:165
  155.2 7.9 %stack.27 = f32[1,4,3,80,1536]{4,3,2,1,0:T(8,128)} reshape(f32[960,12,128]{2,1,0:T(8,128)} %copy.137) | data formatting | bytes 11796480 | tf_op jit(solution)/shard_map/stack | solution.py:166
  163.1 4.8 %fusion.76 = (bf16[2,4,1,80,1536]{4,3,1,2,0:T(8,128)(2,1)}, bf16[2,4,1,80,1536]{4,3,1,2,0:T(8,128)(2,1)}) fusion(f32[1,4,3,80,1536]{4,3,2,1,0:T(8,128)} %stack.27, f32[1,4,3,80,1536]{4,3,2,1,0:T(8,128)} %stack.26), kind=kLoop, calls=%fused_computation.155 | loop fusion | flops 2949120 | bytes 15728640 | tf_op jit(solution)/shard_map/slice | solution.py:167
  169.2 36.2 %collective-permute-start.5 = (bf16[2,4,1,80,1536]{4,3,1,2,0:T(8,128)(2,1)}, bf16[2,4,1,80,1536]{4,3,1,2,0:T(8,128)(2,1)}, u32[]{:S(2)}, u32[]{:S(2)}) collective-permute-start(bf16[2,4,1,80,1536]{4,3,1,2,0:T(8,128)(2,1)} %get-tuple-element.95), channel_id=1, source_target_pairs={{0,1},{1,2},{2,3},{3,4},{4,5},{5,6},{6,7},{7,8},{8,9},{9,10},{10,1... | collective-permute-start | bytes 5898248 | tf_op jit(solution)/shard_map/ppermute | solution.py:17
  213.7 5.2 %fusion.30 = f32[160,4,128]{2,0,1:T(8,128)S(1)} fusion(f32[4,160,960]{2,1,0:T(8,128)} %copy-done.14, f32[4,960,160]{1,2,0:T(8,128)} %fusion.37, bf16[960,4,128]{2,1,0:T(4,128)(2,1)} %copy-done.19), kind=kOutput, calls=%fused_computation.54 | convolution fusion | flops 160360000 | bytes 6225920 | tf_op jit(solution)/shard_map/gqk,kgd->qgd/dot_general | solution.py:98
  218.9 5.2 %fusion.29 = f32[160,4,128]{2,0,1:T(8,128)S(1)} fusion(f32[4,160,960]{2,1,0:T(8,128)} %copy-done.15, f32[4,960,160]{1,2,0:T(8,128)} %fusion.35, bf16[960,4,128]{2,1,0:T(4,128)(2,1)} %get-tuple-element.102), kind=kOutput, calls=%fused_computation.53 | convolution fusion | flops 160360000 | bytes 6225920 | tf_op jit(solution)/shard_map/gqk,kgd->qgd/dot_general | solution.py:98
  224.1 5.8 %fusion.28 = f32[160,4,128]{2,0,1:T(8,128)} fusion(f32[4,160,960]{2,1,0:T(8,128)} %copy-done.16, f32[4,960,160]{1,2,0:T(8,128)} %fusion.33, bf16[960,4,128]{2,1,0:T(4,128)(2,1)} %get-tuple-element.103), kind=kOutput, calls=%fused_computation.52 | convolution fusion | flops 160360000 | bytes 6225920 | tf_op jit(solution)/shard_map/gqk,kgd->qgd/dot_general | solution.py:98
  232.6 6.2 %fusion.74 = (bf16[2,4,1,80,1536]{4,3,1,2,0:T(8,128)(2,1)S(1)}, f32[2,4,1,80,1536]{4,3,1,2,0:T(8,128)}) fusion(bf16[2,4,1,80,1536]{4,3,1,2,0:T(8,128)(2,1)} %collective-permute-done.5, bf16[2,4,1,80,1536]{4,3,1,2,0:T(8,128)(2,1)} %collective-permute-done.4, f32[1,4,3,80,1536]{4,3,2,1,0:T(8,128)} %stack.27, f32[1,4,3,80,1536]{4,3,2,1,0:T(8,128)} %stack.26), kind=kLoop, calls=%fused_computation.154 | loop fusion | flops 7864320 | bytes 21626880 | tf_op jit(solution)/shard_map/convert.5
  246.4 3.1 multiply_reduce_fusion.4
  249.5 6.3 %collective-permute-start.7 = (bf16[2,1,1,80,1536]{4,3,1,2,0:T(8,128)(2,1)}, bf16[2,1,1,80,1536]{4,3,1,2,0:T(8,128)(2,1)S(1)}, u32[]{:S(2)}, u32[]{:S(2)}) collective-permute-start(bf16[2,1,1,80,1536]{4,3,1,2,0:T(8,128)(2,1)} %get-tuple-element.108), channel_id=1, source_target_pairs={{0,64},{64,128},{128,192},{192,256},{256,320},{320,384},{384,448},... | collective-permute-start | bytes 1474568 | tf_op jit(solution)/shard_map/ppermute | solution.py:17
  257.5 11.1 %collective-permute-done.7 = bf16[2,1,1,80,1536]{4,3,1,2,0:T(8,128)(2,1)S(1)} collective-permute-done((bf16[2,1,1,80,1536]{4,3,1,2,0:T(8,128)(2,1)}, bf16[2,1,1,80,1536]{4,3,1,2,0:T(8,128)(2,1)S(1)}, u32[]{:S(2)}, u32[]{:S(2)}) %collective-permute-start.7) | collective-permute-done | bytes 491552 | tf_op jit(solution)/shard_map/ppermute | solution.py:17
  270.0 150.1 %all-reduce = f32[2,128]{1,0:T(2,128)S(1)} all-reduce(f32[2,128]{1,0:T(2,128)S(1)} %pad_maximum_fusion.7), channel_id=2, replica_groups=mesh['tm'=8,'height'=64] {'height'}, use_global_device_ids=true, to_apply=%region_14.15.clone | all-reduce | flops 256 | bytes 2048
  421.0 23.0 %psum.7 = f32[2,2]{1,0:T(2,128)} all-reduce(f32[2,2]{1,0:T(2,128)S(1)} %constant_dynamic-slice_fusion), channel_id=1, replica_groups=mesh['tm'=8,'height'=64] {'tm'}, use_global_device_ids=true, to_apply=%region_15.16 | all-reduce | flops 4 | bytes 32 | tf_op jit(solution)/shard_map/psum | solution.py:194
  (165 shorter events, 82.1 us)
Async XLA Ops:
  3.7 4.9 %copy-start.1 = (f32[160,12,128]{2,1,0:T(8,128)}, f32[160,12,128]{2,1,0:T(8,128)S(1)}, u32[]{:S(2)}) copy-start(f32[160,12,128]{2,1,0:T(8,128)S(1)} %mul.208) | copy-start | bytes 2949124
  8.5 25.7 %collective-permute-start = (bf16[2,1,1,80,1536]{4,3,1,2,0:T(8,128)(2,1)}, bf16[2,1,1,80,1536]{4,3,1,2,0:T(8,128)(2,1)}, u32[]{:S(2)}, u32[]{:S(2)}) collective-permute-start(bf16[2,1,1,80,1536]{4,3,1,2,0:T(8,128)(2,1)} %get-tuple-element.112), channel_id=1, source_target_pairs={{0,64},{64,128},{128,192},{192,256},{256,320},{320,384},{384,448},... | collective-permute-start | bytes 1474568 | tf_op jit(solution)/shard_map/ppermute | solution.py:27
  11.8 22.4 %copy-start.8 = (bf16[1,2,1,80,1536]{4,3,1,2,0:T(8,128)(2,1)S(1)}, bf16[1,2,1,80,1536]{4,3,1,2,0:T(8,128)(2,1)}, u32[]{:S(2)}) copy-start(bf16[1,2,1,80,1536]{4,3,1,2,0:T(8,128)(2,1)} %copy-done.7) | copy-start | bytes 1474564
  11.8 22.4 %collective-permute-start.1 = (bf16[2,1,1,80,1536]{4,3,1,2,0:T(8,128)(2,1)}, bf16[2,1,1,80,1536]{4,3,1,2,0:T(8,128)(2,1)}, u32[]{:S(2)}, u32[]{:S(2)}) collective-permute-start(bf16[2,1,1,80,1536]{4,3,1,2,0:T(8,128)(2,1)} %get-tuple-element.113), channel_id=1, source_target_pairs={{64,0},{128,64},{192,128},{256,192},{320,256},{384,320},{448,384},... | collective-permute-start | bytes 1474568 | tf_op jit(solution)/shard_map/ppermute | solution.py:28
  23.2 22.5 %copy-start.24 = (s32[12,3]{0,1:T(4,128)S(1)}, s32[12,3]{0,1:T(4,128)}, u32[]{:S(2)}) copy-start(s32[12,3]{0,1:T(4,128)} %param.25) | copy-start | bytes 436
  37.2 13.8 %copy-start.25 = (f32[128]{0:T(128)S(1)}, f32[128]{0:T(128)}, u32[]{:S(2)}) copy-start(f32[128]{0:T(128)} %param.23) | copy-start | bytes 1540
  37.2 15.0 %collective-permute-start.3 = (bf16[2,4,1,80,1536]{4,3,1,2,0:T(8,128)(2,1)}, bf16[2,4,1,80,1536]{4,3,1,2,0:T(8,128)(2,1)}, u32[]{:S(2)}, u32[]{:S(2)}) collective-permute-start(bf16[2,4,1,80,1536]{4,3,1,2,0:T(8,128)(2,1)} %pad_maximum_fusion.4), channel_id=1, source_target_pairs={{1,0},{2,1},{3,2},{4,3},{5,4},{6,5},{7,6},{8,7},{9,8},{10,9},{11,1... | collective-permute-start | bytes 5898248 | tf_op jit(solution)/shard_map/ppermute | solution.py:28
  38.6 13.5 %collective-permute-start.2 = (bf16[2,4,1,80,1536]{4,3,1,2,0:T(8,128)(2,1)}, bf16[2,4,1,80,1536]{4,3,1,2,0:T(8,128)(2,1)}, u32[]{:S(2)}, u32[]{:S(2)}) collective-permute-start(bf16[2,4,1,80,1536]{4,3,1,2,0:T(8,128)(2,1)} %pad_maximum_fusion.4), channel_id=1, source_target_pairs={{0,1},{1,2},{2,3},{3,4},{4,5},{5,6},{6,7},{7,8},{8,9},{9,10},{10,1... | collective-permute-start | bytes 5898248 | tf_op jit(solution)/shard_map/ppermute | solution.py:27
  45.7 6.5 %copy-start.9 = (bf16[2,1,80,1536]{3,2,1,0:T(8,128)(2,1)S(1)}, bf16[2,1,80,1536]{3,2,1,0:T(8,128)(2,1)}, u32[]{:S(2)}) copy-start(bf16[2,1,80,1536]{3,2,1,0:T(8,128)(2,1)} %param.21) | copy-start | bytes 1474564
  66.1 5.2 %copy-start.2 = (bf16[1,4,3,80,1536]{4,3,1,2,0:T(8,128)(2,1)S(1)}, bf16[1,4,3,80,1536]{4,3,1,2,0:T(8,128)(2,1)}, u32[]{:S(2)}) copy-start(bf16[1,4,3,80,1536]{4,3,1,2,0:T(8,128)(2,1)} %get-tuple-element.97) | copy-start | bytes 8847364
  79.5 5.2 %copy-start.20 = (s32[160,960]{1,0:T(8,128)S(1)}, s32[160,960]{1,0:T(8,128)}, u32[]{:S(2)}) copy-start(s32[160,960]{1,0:T(8,128)} %subtract_abs_fusion.1) | copy-start | bytes 1843204
  79.5 5.2 %copy-start.21 = (s32[160,960]{1,0:T(8,128)S(1)}, s32[160,960]{1,0:T(8,128)}, u32[]{:S(2)}) copy-start(s32[160,960]{1,0:T(8,128)} %subtract_abs_fusion) | copy-start | bytes 1843204
  79.5 5.2 %copy-start.22 = (bf16[160,12,128]{2,0,1:T(8,128)(2,1)S(1)}, bf16[160,12,128]{2,0,1:T(8,128)(2,1)}, u32[]{:S(2)}) copy-start(bf16[160,12,128]{2,0,1:T(8,128)(2,1)} %multiply_convert_fusion.1) | copy-start | bytes 1474564
  79.5 5.2 %copy-start.27 = (pred[960]{0:T(1024)(128)(4,1)S(1)}, pred[960]{0:T(1024)(128)(4,1)}, u32[]{:S(2)}) copy-start(pred[960]{0:T(1024)(128)(4,1)} %and_and_fusion) | copy-start | bytes 2884
  79.6 5.2 %copy-start.32 = (s32[4]{0:T(128)S(1)}, s32[4]{0:T(128)}, u32[]{:S(2)}) copy-start(s32[4]{0:T(128)} %get-tuple-element.117) | copy-start | bytes 52
  79.6 5.2 %copy-start.33 = (s32[4]{0:T(128)S(1)}, s32[4]{0:T(128)}, u32[]{:S(2)}) copy-start(s32[4]{0:T(128)} %get-tuple-element.122) | copy-start | bytes 52
  79.6 5.2 %copy-start.34 = (s32[4]{0:T(128)S(1)}, s32[4]{0:T(128)}, u32[]{:S(2)}) copy-start(s32[4]{0:T(128)} %get-tuple-element.123) | copy-start | bytes 52
  91.6 6.6 %copy-start.23 = (bf16[160,12,128]{2,0,1:T(8,128)(2,1)S(1)}, bf16[160,12,128]{2,0,1:T(8,128)(2,1)}, u32[]{:S(2)}) copy-start(bf16[160,12,128]{2,0,1:T(8,128)(2,1)} %multiply_convert_fusion.1) | copy-start | bytes 1474564
  106.3 6.6 %copy-start.28 = (pred[960]{0:T(1024)(128)(4,1)S(1)}, pred[960]{0:T(1024)(128)(4,1)}, u32[]{:S(2)}) copy-start(pred[960]{0:T(1024)(128)(4,1)} %and_and_fusion) | copy-start | bytes 2884
  106.3 6.6 %copy-start.29 = (s32[4]{0:T(128)S(1)}, s32[4]{0:T(128)}, u32[]{:S(2)}) copy-start(s32[4]{0:T(128)} %get-tuple-element.118) | copy-start | bytes 52
  106.3 6.6 %copy-start.30 = (s32[4]{0:T(128)S(1)}, s32[4]{0:T(128)}, u32[]{:S(2)}) copy-start(s32[4]{0:T(128)} %get-tuple-element.124) | copy-start | bytes 52
  106.3 6.6 %copy-start.31 = (s32[4]{0:T(128)S(1)}, s32[4]{0:T(128)}, u32[]{:S(2)}) copy-start(s32[4]{0:T(128)} %get-tuple-element.125) | copy-start | bytes 52
  167.9 64.7 %collective-permute-start.4 = (bf16[2,4,1,80,1536]{4,3,1,2,0:T(8,128)(2,1)}, bf16[2,4,1,80,1536]{4,3,1,2,0:T(8,128)(2,1)}, u32[]{:S(2)}, u32[]{:S(2)}) collective-permute-start(bf16[2,4,1,80,1536]{4,3,1,2,0:T(8,128)(2,1)} %get-tuple-element.94), channel_id=1, source_target_pairs={{1,0},{2,1},{3,2},{4,3},{5,4},{6,5},{7,6},{8,7},{9,8},{10,9},{11,1... | collective-permute-start | bytes 5898248 | tf_op jit(solution)/shard_map/ppermute | solution.py:17
  169.2 63.4 %collective-permute-start.5 = (bf16[2,4,1,80,1536]{4,3,1,2,0:T(8,128)(2,1)}, bf16[2,4,1,80,1536]{4,3,1,2,0:T(8,128)(2,1)}, u32[]{:S(2)}, u32[]{:S(2)}) collective-permute-start(bf16[2,4,1,80,1536]{4,3,1,2,0:T(8,128)(2,1)} %get-tuple-element.95), channel_id=1, source_target_pairs={{0,1},{1,2},{2,3},{3,4},{4,5},{5,6},{6,7},{7,8},{8,9},{9,10},{10,1... | collective-permute-start | bytes 5898248 | tf_op jit(solution)/shard_map/ppermute | solution.py:17
  239.8 16.5 %collective-permute-start.6 = (bf16[2,1,1,80,1536]{4,3,1,2,0:T(8,128)(2,1)}, bf16[2,1,1,80,1536]{4,3,1,2,0:T(8,128)(2,1)}, u32[]{:S(2)}, u32[]{:S(2)}) collective-permute-start(bf16[2,1,1,80,1536]{4,3,1,2,0:T(8,128)(2,1)} %get-tuple-element.109), channel_id=1, source_target_pairs={{64,0},{128,64},{192,128},{256,192},{320,256},{384,320},{448,384},... | collective-permute-start | bytes 1474568 | tf_op jit(solution)/shard_map/ppermute | solution.py:17
  246.4 9.4 %copy-start = (f32[2,4,1,80,1536]{4,3,1,2,0:T(8,128)S(1)}, f32[2,4,1,80,1536]{4,3,1,2,0:T(8,128)}, u32[]{:S(2)}) copy-start(f32[2,4,1,80,1536]{4,3,1,2,0:T(8,128)} %get-tuple-element.93) | copy-start | bytes 11796484
  249.5 19.1 %collective-permute-start.7 = (bf16[2,1,1,80,1536]{4,3,1,2,0:T(8,128)(2,1)}, bf16[2,1,1,80,1536]{4,3,1,2,0:T(8,128)(2,1)S(1)}, u32[]{:S(2)}, u32[]{:S(2)}) collective-permute-start(bf16[2,1,1,80,1536]{4,3,1,2,0:T(8,128)(2,1)} %get-tuple-element.108), channel_id=1, source_target_pairs={{0,64},{64,128},{128,192},{192,256},{256,320},{320,384},{384,448},... | collective-permute-start | bytes 1474568 | tf_op jit(solution)/shard_map/ppermute | solution.py:17
  255.9 12.9 %copy-start.3 = (f32[1,2,1,80,1536]{4,3,1,2,0:T(8,128)S(1)}, f32[1,2,1,80,1536]{4,3,1,2,0:T(8,128)}, u32[]{:S(2)}) copy-start(f32[1,2,1,80,1536]{4,3,1,2,0:T(8,128)} %mul.209) | copy-start | bytes 2949124
  255.9 12.9 %copy-start.5 = (bf16[2,1,80,1536]{3,2,1,0:T(8,128)(2,1)S(1)}, bf16[2,1,80,1536]{3,2,1,0:T(8,128)(2,1)}, u32[]{:S(2)}) copy-start(bf16[2,1,80,1536]{3,2,1,0:T(8,128)(2,1)} %param.20) | copy-start | bytes 1474564
  268.8 177.5 %copy-start.26 = (f32[128]{0:T(128)S(1)}, f32[128]{0:T(128)}, u32[]{:S(2)}) copy-start(f32[128]{0:T(128)} %param.24) | copy-start | bytes 1540
  449.1 5.1 %copy-start.6 = (bf16[2,1,80,1536]{3,2,1,0:T(8,128)(2,1)S(1)}, bf16[2,1,80,1536]{3,2,1,0:T(8,128)(2,1)}, u32[]{:S(2)}) copy-start(bf16[2,1,80,1536]{3,2,1,0:T(8,128)(2,1)} %param.20) | copy-start | bytes 1474564
  449.1 5.1 %copy-start.13 = (f32[2,1,80,1536]{3,2,0,1:T(8,128)S(1)}, f32[2,1,80,1536]{3,2,0,1:T(8,128)}, u32[]{:S(2)}) copy-start(f32[2,1,80,1536]{3,2,0,1:T(8,128)} %mul.242) | copy-start | bytes 2949124
  (11 other events, 21.1 us)
where the time goes:
time: 461 us; the launch traced here: 457 us
  blocking collectives  173 us (38%)
  local copies, waits for them, and re-layouts  91.8 us (20%)
  starting transfers between devices  61.7 us (13%)
  matrix products  55.4 us (12%)
  other arithmetic  50.3 us (11%)
  waiting for transfers between devices  22.4 us (5%)
    unnamed x1, blocking collectives  150 us
    ppermute x4, starting transfers between devices, from_behind(): return lax.ppermute(block, axis, route)  45.9 us
    psum x1, blocking collectives, on_device(): gain_grad = lax.psum(owner_part, 'tm')  23 us
    dot_general x3, matrix products, full_pass(): jnp.einsum('gqk,qgd->kgd', score_back, queries, preferred_element_type=jn...  19.6 us
    dot_general x3, matrix products, full_pass(): jnp.einsum('gqk,kgd->qgd', score_back, key_rows, preferred_element_type=j...  16.2 us
    another operation x2, local copies, waits for them, and re-layouts, on_device(): jnp.stack([key_ext, value_ext])  16 us
    slice x3, local copies, waits for them, and re-layouts, head_slice(): return array_rows[:, head_first:head_first + group_size]  12.3 us
    ppermute x4, waiting for transfers between devices, from_behind(): return lax.ppermute(block, axis, route)  11.4 us
  transfers between devices with their start and end apart: 8, of which 3 were waited for; matrix products, arithmetic and copies ran while one was open for 11% of the time, Pallas kernels for 0%

commit v1 on v0

v1 whole, which is shorter than its diff:
```python
import functools

import jax
import jax.numpy as jnp
from jax import lax
from jax.experimental import pallas as pl
from jax.experimental.pallas import tpu as pltpu
from jax.sharding import PartitionSpec as P

TILE_W = 8
EPSILON = 1e-06
HEAD_DIM = 128
LOG2E = 1.4426950408889634
BLOCKED = 1000.0
LANES = 128
BOTH = ("tm", "height")


def rms_inverse(full_rows):
    return lax.rsqrt(jnp.mean(full_rows * full_rows, axis=-1, keepdims=True) + EPSILON)


def norm_backward(grad_rows, unit_rows, inverse, gain_row):
    scaled = grad_rows * gain_row
    return inverse * (scaled - unit_rows * jnp.mean(unit_rows * scaled, axis=-1, keepdims=True))


def pack_kernel(key_ref, value_ref, gain_ref, both_ref, first_ref, last_ref):
    frames, width, _ = key_ref.shape
    gain_row = gain_ref[...]
    edges = (first_ref, last_ref)
    for f in range(frames):
        full_rows = key_ref[f].astype(jnp.float32)
        key_rows = (full_rows * rms_inverse(full_rows) * gain_row).astype(jnp.bfloat16)
        both_ref[f, 0] = key_rows
        both_ref[f, 1] = value_ref[f]
        edges[f][0] = key_rows
        edges[f][1] = value_ref[f]


def head_block(lead):
    zeros = (0,) * len(lead)
    return pl.BlockSpec((*lead, LANES), lambda g: (*zeros, g))


def fixed_block(shape):
    zeros = (0,) * len(shape)
    return pl.BlockSpec(shape, lambda g: zeros)


def smem_block():
    return pl.BlockSpec(memory_space=pltpu.SMEM)


def pack(key_raw, values, key_gain):
    frames, width, channels = key_raw.shape
    heads = channels // LANES
    kinds = jax.ShapeDtypeStruct
    return pl.pallas_call(
        pack_kernel,
        grid=(heads,),
        in_specs=[head_block((frames, width)), head_block((frames, width)), fixed_block((1, LANES))],
        out_specs=[head_block((frames, 2, width)), head_block((2, width)), head_block((2, width))],
        out_shape=[
            kinds((frames, 2, width, channels), jnp.bfloat16),
            kinds((2, width, channels), jnp.bfloat16),
            kinds((2, width, channels), jnp.bfloat16),
        ],
        name="pack_keys_values",
    )(key_raw, values, key_gain)


def padded(count):
    return -(-count // LANES) * LANES


def variants():
    out = {}
    for rows_on in (0, 1):
        for frames_on in (0, 1):
            rows = (0, 1, 2) if rows_on else (0,)
            frames = (0, 1, 2, 3) if frames_on else (1, 2)
            out[rows_on, frames_on] = [(r, e) for r in rows for e in frames]
    return out


def fill_distance(dist_ref, blocks, width, valid_ref):
    queries, keys = dist_ref.shape
    q_ids = lax.broadcasted_iota(jnp.int32, (queries, keys), 0)
    k_ids = lax.broadcasted_iota(jnp.int32, (queries, keys), 1)
    q_frame = (q_ids >= width).astype(jnp.int32)
    q_tile = (q_ids - q_frame * width) // TILE_W
    k_block = jnp.zeros_like(k_ids)
    for i in range(1, len(blocks) + 1):
        k_block += (k_ids >= i * width).astype(jnp.int32)
    k_tile = (k_ids - k_block * width) // TILE_W
    gap = jnp.abs(q_tile - k_tile).astype(jnp.float32)
    reach = 1 if any(e == 0 for _, e in blocks) else 0
    allowed = jnp.zeros((queries, keys), jnp.float32)
    for i, (r, e) in enumerate(blocks):
        here = jnp.logical_and(k_block == i, jnp.abs(q_frame + 1 - e) <= reach)
        ok = jnp.float32(1.0)
        if r == 2:
            ok = ok * valid_ref[0].astype(jnp.float32)
        if e == 0:
            ok = ok * valid_ref[1].astype(jnp.float32)
        if e == 3:
            ok = ok * valid_ref[2].astype(jnp.float32)
        allowed += jnp.where(here, ok, 0.0)
    dist_ref[...] = jnp.where(allowed > 0.5, gap, BLOCKED)


def matmul(a, b, dims):
    return lax.dot_general(a, b, (dims, ((), ())), preferred_element_type=jnp.float32)


def attend_kernel(
    window_ref, valid_ref, query_ref, grad_ref, own_ref, chip_ref, off_ref,
    prev_ref, next_ref, chip_prev_ref, chip_next_ref, off_prev_ref, off_next_ref,
    q_gain_ref, k_gain_ref,
    query_grad_ref, own_out, chip_out, off_out,
    prev_out, next_out, chip_prev_out, chip_next_out, off_prev_out, off_next_out, gain_out,
    key_buf, value_buf, *dist_refs,
):
    step = pl.program_id(0)
    frames, width, head_dim = query_ref.shape
    tokens = frames * width
    table = variants()
    dists = dict(zip(table, dist_refs))
    scale = head_dim ** (-0.5)

    sources = {}
    targets = {}
    rows_in = ((own_ref, prev_ref, next_ref), (chip_ref, chip_prev_ref, chip_next_ref), (off_ref, off_prev_ref, off_next_ref))
    rows_out = ((own_out, prev_out, next_out), (chip_out, chip_prev_out, chip_next_out), (off_out, off_prev_out, off_next_out))
    for r in range(3):
        for refs, where in ((rows_in[r], sources), (rows_out[r], targets)):
            where[r, 0] = refs[1]
            where[r, 1] = refs[0].at[0]
            where[r, 2] = refs[0].at[1]
            where[r, 3] = refs[2]

    @pl.when(step == 0)
    def _():
        key_buf[...] = jnp.zeros_like(key_buf)
        value_buf[...] = jnp.zeros_like(value_buf)
        gain_out[...] = jnp.zeros_like(gain_out)
        for which, blocks in table.items():
            fill_distance(dists[which], blocks, width, valid_ref)

    frame_reach = window_ref[step, 0]
    row_reach = window_ref[step, 1]
    tile_reach = window_ref[step, 2].astype(jnp.float32)

    def work(which):
        blocks = table[which]
        keys = padded(len(blocks) * width)
        for i, block in enumerate(blocks):
            key_buf[i * width : (i + 1) * width] = sources[block][0]
            value_buf[i * width : (i + 1) * width] = sources[block][1]
        gain_row = q_gain_ref[...]
        full_rows = query_ref[...].reshape(tokens, head_dim).astype(jnp.float32)
        inverse = rms_inverse(full_rows)
        unit_rows = full_rows * inverse
        queries = (unit_rows * gain_row).astype(jnp.bfloat16)
        grads = grad_ref[...].reshape(tokens, head_dim)
        key_rows = key_buf[0:keys]
        value_rows = value_buf[0:keys]
        scores = matmul(queries, key_rows, ((1,), (1,)))
        weight = jnp.where(
            dists[which][...] <= tile_reach, jnp.exp2(scores * (scale * LOG2E)), 0.0
        )
        total = jnp.sum(weight, axis=-1, keepdims=True)
        prob = weight * (1.0 / total)
        prob_back = matmul(grads, value_rows, ((1,), (1,)))
        delta = jnp.sum(prob * prob_back, axis=-1, keepdims=True)
        score_back = (prob * ((prob_back - delta) * scale)).astype(jnp.bfloat16)
        query_back = matmul(score_back, key_rows, ((1,), (0,)))
        key_back = matmul(score_back, queries, ((0,), (0,)))
        value_back = matmul(prob.astype(jnp.bfloat16), grads, ((0,), (0,)))
        for i, block in enumerate(blocks):
            out = targets[block]
            out[0] = key_back[i * width : (i + 1) * width].astype(out.dtype)
            out[1] = value_back[i * width : (i + 1) * width].astype(out.dtype)
        for block, out in targets.items():
            if block not in blocks:
                out[...] = jnp.zeros_like(out)
        result = norm_backward(query_back, unit_rows, inverse, gain_row)
        query_grad_ref[...] = result.reshape(frames, width, head_dim).astype(query_grad_ref.dtype)
        gain_out[0:1] += jnp.sum(query_back * unit_rows, axis=0, keepdims=True)
        gain_out[1:2] += jnp.sum(query_back * queries.astype(jnp.float32), axis=0, keepdims=True) / k_gain_ref[...]

    for which in table:
        rows_on, frames_on = which

        @pl.when(jnp.logical_and(row_reach == rows_on, frame_reach == frames_on))
        def _(which=which):
            work(which)


def attend(window, valid, query_raw, out_grad, own, chip, off, edges, query_gain, key_gain):
    frames, width, channels = query_raw.shape
    heads = channels // LANES
    kinds = jax.ShapeDtypeStruct
    token = head_block((frames, width))
    pair = head_block((frames, 2, width))
    edge = head_block((2, width))
    gain = fixed_block((1, LANES))
    pair_shape = (frames, 2, width, channels)
    edge_shape = (2, width, channels)
    most = padded(12 * width)
    return pl.pallas_call(
        attend_kernel,
        grid=(heads,),
        in_specs=[smem_block(), smem_block(), token, token, pair, pair, pair] + [edge] * 6 + [gain, gain],
        out_specs=[token, pair, pair, pair] + [edge] * 6 + [fixed_block((2, LANES))],
        out_shape=[
            kinds(query_raw.shape, jnp.bfloat16),
            kinds(pair_shape, jnp.float32),
            kinds(pair_shape, jnp.bfloat16),
            kinds(pair_shape, jnp.bfloat16),
        ]
        + [kinds(edge_shape, jnp.bfloat16)] * 6
        + [kinds((2, LANES), jnp.float32)],
        scratch_shapes=[
            pltpu.VMEM((most, LANES), jnp.bfloat16),
            pltpu.VMEM((most, LANES), jnp.bfloat16),
        ]
        + [
            pltpu.VMEM((frames * width, padded(len(blocks) * width)), jnp.float32)
            for blocks in variants().values()
        ],
        compiler_params=pltpu.CompilerParams(vmem_limit_bytes=40 * 1024 * 1024),
        name="attend",
    )(window, valid, query_raw, out_grad, own, chip, off, *edges, query_gain, key_gain)


def finish_kernel(
    key_ref, own_ref, chip_ref, off_ref, first_ref, last_ref, off_first_ref, off_last_ref, gain_ref,
    key_grad_ref, value_grad_ref,
):
    frames = key_ref.shape[0]
    gain_row = gain_ref[...]
    edges = ((first_ref, off_first_ref), (last_ref, off_last_ref))
    for f in range(frames):
        sums = []
        for c in range(2):
            terms = own_ref[f, c]
            for ref in (chip_ref.at[f], off_ref.at[f], *edges[f]):
                terms = terms + ref[c].astype(jnp.float32)
            sums.append(terms)
        full_rows = key_ref[f].astype(jnp.float32)
        inverse = rms_inverse(full_rows)
        result = norm_backward(sums[0], full_rows * inverse, inverse, gain_row)
        key_grad_ref[f] = result.astype(key_grad_ref.dtype)
        value_grad_ref[f] = sums[1].astype(value_grad_ref.dtype)


def finish(key_raw, own, chip, off, edges, key_gain):
    frames, width, channels = key_raw.shape
    heads = channels // LANES
    token = head_block((frames, width))
    pair = head_block((frames, 2, width))
    edge = head_block((2, width))
    return pl.pallas_call(
        finish_kernel,
        grid=(heads,),
        in_specs=[token, pair, pair, pair] + [edge] * 4 + [fixed_block((1, LANES))],
        out_specs=[token, token],
        out_shape=[jax.ShapeDtypeStruct(key_raw.shape, jnp.bfloat16)] * 2,
        name="finish_keys",
    )(key_raw, own, chip, off, *edges, key_gain)


def off_chip(h):
    return h + 1 if h % 2 else h - 1


def move(block, frame_step, row_rule):
    frames_size, rows_size = lax.axis_size("tm"), lax.axis_size("height")
    route = []
    for t in range(frames_size):
        for h in range(rows_size):
            to_t, to_h = t + frame_step, row_rule(h)
            if 0 <= to_t < frames_size and 0 <= to_h < rows_size:
                route.append((t * rows_size + h, to_t * rows_size + to_h))
    return lax.ppermute(block, BOTH, route)


def same_row(h):
    return h


def chip_row(h):
    return h ^ 1


def on_device(query_raw, key_raw, values, out_grad, query_gain, key_gain, window):
    frames, _, width, channels = query_raw.shape
    flat = (frames, width, channels)
    t, h = lax.axis_index("tm"), lax.axis_index("height")
    t_size, h_size = lax.axis_size("tm"), lax.axis_size("height")
    partner = jnp.where(h % 2 == 1, h + 1, h - 1)
    valid = jnp.stack(
        [jnp.logical_and(partner >= 0, partner < h_size), t > 0, t < t_size - 1]
    ).astype(jnp.int32)
    q_gain, k_gain = query_gain[None], key_gain[None]
    key_flat = key_raw.reshape(flat)
    own, first, last = pack(key_flat, values.reshape(flat), k_gain)

    prev = move(last, 1, same_row)
    following = move(first, -1, same_row)
    off = move(own, 0, off_chip)
    chip = move(own, 0, chip_row)
    off_prev = move(last, 1, off_chip)
    off_next = move(first, -1, off_chip)
    chip_prev = move(prev, 0, chip_row)
    chip_next = move(following, 0, chip_row)

    (
        query_grad, own_sum, chip_sum, off_sum,
        prev_sum, next_sum, chip_prev_sum, chip_next_sum, off_prev_sum, off_next_sum, gain_part,
    ) = attend(
        window, valid, query_raw.reshape(flat), out_grad.reshape(flat), own, chip, off,
        (prev, following, chip_prev, chip_next, off_prev, off_next), q_gain, k_gain,
    )

    def add(a, b):
        return (a.astype(jnp.float32) + b.astype(jnp.float32)).astype(jnp.bfloat16)

    prev_all = add(prev_sum, move(chip_prev_sum, 0, chip_row))
    next_all = add(next_sum, move(chip_next_sum, 0, chip_row))
    off_back = move(off_sum, 0, off_chip)
    last_back = move(prev_all, -1, same_row)
    first_back = move(next_all, 1, same_row)
    off_last_back = move(off_prev_sum, -1, off_chip)
    off_first_back = move(off_next_sum, 1, off_chip)
    chip_back = move(chip_sum, 0, chip_row)

    per_row = LANES // h_size
    pieces = gain_part.reshape(2, h_size, per_row).transpose(1, 0, 2).reshape(1, h_size, 2 * per_row)
    pieces = jnp.broadcast_to(pieces, (t_size, h_size, 2 * per_row)).reshape(t_size * h_size, 2 * per_row)
    gain_grad = lax.all_to_all(pieces, BOTH, 0, 0, tiled=True).sum(0).reshape(2, per_row)

    key_grad, value_grad = finish(
        key_flat, own_sum, chip_back, off_back, (first_back, last_back, off_first_back, off_last_back), k_gain
    )
    shape = query_raw.shape
    return (query_grad.reshape(shape), key_grad.reshape(shape), value_grad.reshape(shape), gain_grad)


def solution(mesh):
    token = P("tm", "height", None, None)
    return jax.shard_map(
        on_device,
        mesh=mesh,
        in_specs=(token, token, token, token, P(), P(), P()),
        out_specs=(token, token, token, P(None, "height")),
        check_vma=False,
    )
```

time: 461 us -> 195 us (0.42)
  the two profiles are of different devices: /device:TPU:8 before, /device:TPU:1 now
where the time goes in v1:
time: 195 us; the launch traced here: 194 us
  blocking collectives  54.4 us (28%)
  waiting for transfers between devices  49.1 us (25%)
  starting transfers between devices  47.2 us (24%)
  Pallas kernels  30.6 us (16%)
  local copies, waits for them, and re-layouts  9.02 us (5%)
  other arithmetic  2.42 us (1%)
    all_to_all x1, blocking collectives, on_device(): lax.all_to_all(pieces, BOTH, 0, 0, tiled=True).sum(0).reshape(2, per_row)  54.4 us
    ppermute x16, waiting for transfers between devices, move(): return lax.ppermute(block, BOTH, route)  49.1 us
    ppermute x16, starting transfers between devices, move(): return lax.ppermute(block, BOTH, route)  47.2 us
    pallas_call x1, Pallas kernels, attend(): pl.pallas_call(attend_kernel, grid=(heads,), in_specs=[smem_block(), smem...  14.6 us
    pallas_call x1, Pallas kernels, finish(): pl.pallas_call(finish_kernel, grid=(heads,), in_specs=[token, pair, pair,...  8.79 us
    unnamed x21, local copies, waits for them, and re-layouts  8.04 us
    pallas_call x1, Pallas kernels, pack(): pl.pallas_call(pack_kernel, grid=(heads,), in_specs=[head_block((frames,...  7.31 us
  transfers between devices with their start and end apart: 16, of which 5 were waited for; matrix products, arithmetic and copies ran while one was open for 2% of the time, Pallas kernels for 0%

profile of v1, /device:TPU:1, one launch (start us, length us, event | category | flops | bytes accessed | tf_op | source)
XLA Modules:
  0.0 193.7 jit_solution(18340884145793505265)
XLA Ops:
  0.6 7.3 %pack_keys_values.1 = (bf16[2,2,80,1536]{3,2,1,0:T(8,128)(2,1)}, bf16[2,80,1536]{2,1,0:T(8,128)(2,1)}, bf16[2,80,1536]{2,1,0:T(8,128)(2,1)}) custom-call(bf16[2,80,1536]{2,1,0:T(8,128)(2,1)} %bitcast.27, bf16[2,80,1536]{2,1,0:T(8,128)(2,1)} %bitcast.30, f32[1,128]{1,0:T(1,128)} %bitcast.23), custom_call_target="tpu_custom_call" | custom-call | tf_op jit(solution)/shard_map/pack_keys_values/pallas_call | solution.py:59
  7.9 6.0 %collective-permute-start.6 = (bf16[2,80,1536]{2,1,0:T(8,128)(2,1)}, bf16[2,80,1536]{2,1,0:T(8,128)(2,1)S(1)}, u32[]{:S(2)}, u32[]{:S(2)}) collective-permute-start(bf16[2,80,1536]{2,1,0:T(8,128)(2,1)} %get-tuple-element.21), channel_id=1, source_target_pairs={{1,66},{2,65},{3,68},{4,67},{5,70},{6,69},{7,72},{8,71},{9,74},{10... | collective-permute-start | bytes 1474568 | tf_op jit(solution)/shard_map/ppermute | solution.py:287
  14.0 2.7 %collective-permute-start.2 = (bf16[2,80,1536]{2,1,0:T(8,128)(2,1)}, bf16[2,80,1536]{2,1,0:T(8,128)(2,1)S(1)}, u32[]{:S(2)}, u32[]{:S(2)}) collective-permute-start(bf16[2,80,1536]{2,1,0:T(8,128)(2,1)} %get-tuple-element.21), channel_id=1, source_target_pairs={{0,64},{1,65},{2,66},{3,67},{4,68},{5,69},{6,70},{7,71},{8,72},{9,... | collective-permute-start | bytes 1474568 | tf_op jit(solution)/shard_map/ppermute | solution.py:287
  16.7 1.3 collective-permute-start.3
  18.0 3.2 %collective-permute-start.1 = (bf16[2,2,80,1536]{3,2,1,0:T(8,128)(2,1)}, bf16[2,2,80,1536]{3,2,1,0:T(8,128)(2,1)S(1)}, u32[]{:S(2)}, u32[]{:S(2)}) collective-permute-start(bf16[2,2,80,1536]{3,2,1,0:T(8,128)(2,1)} %get-tuple-element.20.own_ref), channel_id=1, source_target_pairs={{1,2},{2,1},{3,4},{4,3},{5,6},{6,5},{7,8},{8,7},{9,10},{10,9},{11,... | collective-permute-start | bytes 2949128 | tf_op jit(solution)/shard_map/ppermute | solution.py:287
  21.2 1.9 collective-permute-start
  23.1 2.2 %collective-permute-done.6.off_prev_ref = bf16[2,80,1536]{2,1,0:T(8,128)(2,1)S(1)} collective-permute-done((bf16[2,80,1536]{2,1,0:T(8,128)(2,1)}, bf16[2,80,1536]{2,1,0:T(8,128)(2,1)S(1)}, u32[]{:S(2)}, u32[]{:S(2)}) %collective-permute-start.6) | collective-permute-done | bytes 491552 | tf_op jit(solution)/shard_map/ppermute | solution.py:287
  25.3 1.3 collective-permute-start.7
  26.6 22.2 %collective-permute-done.2.prev_ref = bf16[2,80,1536]{2,1,0:T(8,128)(2,1)S(1)} collective-permute-done((bf16[2,80,1536]{2,1,0:T(8,128)(2,1)}, bf16[2,80,1536]{2,1,0:T(8,128)(2,1)S(1)}, u32[]{:S(2)}, u32[]{:S(2)}) %collective-permute-start.2) | collective-permute-done | bytes 491552 | tf_op jit(solution)/shard_map/ppermute | solution.py:287
  48.7 2.9 %collective-permute-start.4 = (bf16[2,80,1536]{2,1,0:T(8,128)(2,1)S(1)}, bf16[2,80,1536]{2,1,0:T(8,128)(2,1)}, u32[]{:S(2)}, u32[]{:S(2)}) collective-permute-start(bf16[2,80,1536]{2,1,0:T(8,128)(2,1)S(1)} %collective-permute-done.2.prev_ref), channel_id=1, source_target_pairs={{0,1},{1,0},{2,3},{3,2},{4,5},{5,4},{6,7},{7,6},{8,9},{9,8},{10,11... | collective-permute-start | bytes 1474568 | tf_op jit(solution)/shard_map/ppermute | solution.py:287
  51.7 1.9 collective-permute-start.5
  53.7 0.8 copy.21.window_ref
  54.5 1.1 collective-permute-done.5.chip_next_ref
  55.6 4.1 %collective-permute-done.1.off_ref = bf16[2,2,80,1536]{3,2,1,0:T(8,128)(2,1)S(1)} collective-permute-done((bf16[2,2,80,1536]{3,2,1,0:T(8,128)(2,1)}, bf16[2,2,80,1536]{3,2,1,0:T(8,128)(2,1)S(1)}, u32[]{:S(2)}, u32[]{:S(2)}) %collective-permute-start.1) | collective-permute-done | bytes 983072 | tf_op jit(solution)/shard_map/ppermute | solution.py:287
  59.7 1.2 copy-done.1
  60.9 1.0 copy-done.2
  61.9 1.0 copy-done.3
  64.2 14.6 %attend.1 = (bf16[2,80,1536]{2,1,0:T(8,128)(2,1)}, f32[2,2,80,1536]{3,2,1,0:T(8,128)S(1)}, bf16[2,2,80,1536]{3,2,1,0:T(8,128)(2,1)}, bf16[2,2,80,1536]{3,2,1,0:T...) custom-call(s32[12,3]{1,0:T(8,128)S(1)} %copy.21.window_ref, ...), custom_call_target="tpu_custom_call" | custom-call | tf_op jit(solution)/shard_map/attend/pallas_call | solution.py:212
  78.8 1.3 copy-done
  80.1 1.9 collective-permute-start.10
  82.0 2.4 %collective-permute-start.12 = (bf16[2,80,1536]{2,1,0:T(8,128)(2,1)S(1)}, bf16[2,80,1536]{2,1,0:T(8,128)(2,1)S(1)}, u32[]{:S(2)}, u32[]{:S(2)}) collective-permute-start(bf16[2,80,1536]{2,1,0:T(8,128)(2,1)S(1)} %get-tuple-element.30), channel_id=1, source_target_pairs={{0,1},{1,0},{2,3},{3,2},{4,5},{5,4},{6,7},{7,6},{8,9},{9,8},{10,11... | collective-permute-start | bytes 1474568 | tf_op jit(solution)/shard_map/ppermute | solution.py:287
  84.4 3.6 %collective-permute-start.14 = (bf16[2,80,1536]{2,1,0:T(8,128)(2,1)S(1)}, bf16[2,80,1536]{2,1,0:T(8,128)(2,1)S(1)}, u32[]{:S(2)}, u32[]{:S(2)}) collective-permute-start(bf16[2,80,1536]{2,1,0:T(8,128)(2,1)S(1)} %get-tuple-element.31), channel_id=1, source_target_pairs={{1,66},{2,65},{3,68},{4,67},{5,70},{6,69},{7,72},{8,71},{9,74},{10... | collective-permute-start | bytes 1474568 | tf_op jit(solution)/shard_map/ppermute | solution.py:287
  88.0 1.3 collective-permute-start.15
  89.3 1.9 collective-permute-start.8
  91.2 6.5 %collective-permute-start.9 = (bf16[2,2,80,1536]{3,2,1,0:T(8,128)(2,1)}, bf16[2,2,80,1536]{3,2,1,0:T(8,128)(2,1)S(1)}, u32[]{:S(2)}, u32[]{:S(2)}) collective-permute-start(bf16[2,2,80,1536]{3,2,1,0:T(8,128)(2,1)} %get-tuple-element.26), channel_id=1, source_target_pairs={{1,2},{2,1},{3,4},{4,3},{5,6},{6,5},{7,8},{8,7},{9,10},{10,9},{11,... | collective-permute-start | bytes 2949128 | tf_op jit(solution)/shard_map/ppermute | solution.py:287
  97.7 0.9 add_convert_fusion.1
  98.6 7.1 %collective-permute-start.11 = (bf16[2,80,1536]{2,1,0:T(8,128)(2,1)}, bf16[2,80,1536]{2,1,0:T(8,128)(2,1)}, u32[]{:S(2)}, u32[]{:S(2)}) collective-permute-start(bf16[2,80,1536]{2,1,0:T(8,128)(2,1)} %add_convert_fusion.1), channel_id=1, source_target_pairs={{0,64},{1,65},{2,66},{3,67},{4,68},{5,69},{6,70},{7,71},{8,72},{9,... | collective-permute-start | bytes 1474568 | tf_op jit(solution)/shard_map/ppermute | solution.py:287
  105.7 0.9 add_convert_fusion
  106.6 19.6 %collective-permute-done.14.off_first_ref = bf16[2,80,1536]{2,1,0:T(8,128)(2,1)S(1)} collective-permute-done((bf16[2,80,1536]{2,1,0:T(8,128)(2,1)S(1)}, bf16[2,80,1536]{2,1,0:T(8,128)(2,1)S(1)}, u32[]{:S(2)}, u32[]{:S(2)}) %collective-permute-start.14) | collective-permute-done | bytes 491552 | tf_op jit(solution)/shard_map/ppermute | solution.py:287
  126.2 1.3 collective-permute-start.13
  127.8 54.4 %all_to_all.9 = f32[512,1,4]{2,1,0:T(1,128)S(1)} all-to-all(f32[512,1,4]{2,1,0:T(1,128)S(1)} %bitcast.29), channel_id=1, replica_groups=mesh['tm'=8,'height'=64] {'tm','height'}, dimensions={0} | all-to-all | bytes 16384 | tf_op jit(solution)/shard_map/all_to_all | solution.py:343
  184.9 8.8 %finish_keys.1 = (bf16[2,80,1536]{2,1,0:T(8,128)(2,1)}, bf16[2,80,1536]{2,1,0:T(8,128)(2,1)}) custom-call(bf16[2,80,1536]{2,1,0:T(8,128)(2,1)} %bitcast.28, f32[2,2,80,1536]{3,2,1,0:T(8,128)} %copy-done, bf16[2,2,80,1536]{3,2,1,0:T(8,128)(2,1)} %copy-done.6, bf16[2,2,80,1536]{3,2,1,0:T(8,128)(2,1)} %copy-done.7, ...), custom_call_target="tpu_custom_call" | custom-call | tf_op jit(solution)/shard_map/finish_keys/pallas_call | solution.py:265
  (34 shorter events, 4.4 us)
Async XLA Ops:
  7.9 17.4 %collective-permute-start.6 = (bf16[2,80,1536]{2,1,0:T(8,128)(2,1)}, bf16[2,80,1536]{2,1,0:T(8,128)(2,1)S(1)}, u32[]{:S(2)}, u32[]{:S(2)}) collective-permute-start(bf16[2,80,1536]{2,1,0:T(8,128)(2,1)} %get-tuple-element.21), channel_id=1, source_target_pairs={{1,66},{2,65},{3,68},{4,67},{5,70},{6,69},{7,72},{8,71},{9,74},{10... | collective-permute-start | bytes 1474568 | tf_op jit(solution)/shard_map/ppermute | solution.py:287
  14.0 34.8 %collective-permute-start.2 = (bf16[2,80,1536]{2,1,0:T(8,128)(2,1)}, bf16[2,80,1536]{2,1,0:T(8,128)(2,1)S(1)}, u32[]{:S(2)}, u32[]{:S(2)}) collective-permute-start(bf16[2,80,1536]{2,1,0:T(8,128)(2,1)} %get-tuple-element.21), channel_id=1, source_target_pairs={{0,64},{1,65},{2,66},{3,67},{4,68},{5,69},{6,70},{7,71},{8,72},{9,... | collective-permute-start | bytes 1474568 | tf_op jit(solution)/shard_map/ppermute | solution.py:287
  16.7 35.0 %collective-permute-start.3 = (bf16[2,80,1536]{2,1,0:T(8,128)(2,1)}, bf16[2,80,1536]{2,1,0:T(8,128)(2,1)S(1)}, u32[]{:S(2)}, u32[]{:S(2)}) collective-permute-start(bf16[2,80,1536]{2,1,0:T(8,128)(2,1)} %get-tuple-element.22), channel_id=1, source_target_pairs={{64,0},{65,1},{66,2},{67,3},{68,4},{69,5},{70,6},{71,7},{72,8},{73... | collective-permute-start | bytes 1474568 | tf_op jit(solution)/shard_map/ppermute | solution.py:287
  18.0 41.7 %collective-permute-start.1 = (bf16[2,2,80,1536]{3,2,1,0:T(8,128)(2,1)}, bf16[2,2,80,1536]{3,2,1,0:T(8,128)(2,1)S(1)}, u32[]{:S(2)}, u32[]{:S(2)}) collective-permute-start(bf16[2,2,80,1536]{3,2,1,0:T(8,128)(2,1)} %get-tuple-element.20.own_ref), channel_id=1, source_target_pairs={{1,2},{2,1},{3,4},{4,3},{5,6},{6,5},{7,8},{8,7},{9,10},{10,9},{11,... | collective-permute-start | bytes 2949128 | tf_op jit(solution)/shard_map/ppermute | solution.py:287
  21.2 38.5 %collective-permute-start = (bf16[2,2,80,1536]{3,2,1,0:T(8,128)(2,1)}, bf16[2,2,80,1536]{3,2,1,0:T(8,128)(2,1)S(1)}, u32[]{:S(2)}, u32[]{:S(2)}) collective-permute-start(bf16[2,2,80,1536]{3,2,1,0:T(8,128)(2,1)} %get-tuple-element.20.own_ref), channel_id=1, source_target_pairs={{0,1},{1,0},{2,3},{3,2},{4,5},{5,4},{6,7},{7,6},{8,9},{9,8},{10,11... | collective-permute-start | bytes 2949128 | tf_op jit(solution)/shard_map/ppermute | solution.py:287
  25.3 29.2 %collective-permute-start.7 = (bf16[2,80,1536]{2,1,0:T(8,128)(2,1)}, bf16[2,80,1536]{2,1,0:T(8,128)(2,1)}, u32[]{:S(2)}, u32[]{:S(2)}) collective-permute-start(bf16[2,80,1536]{2,1,0:T(8,128)(2,1)} %get-tuple-element.22), channel_id=1, source_target_pairs={{65,2},{66,1},{67,4},{68,3},{69,6},{70,5},{71,8},{72,7},{73,10},{7... | collective-permute-start | bytes 1474568 | tf_op jit(solution)/shard_map/ppermute | solution.py:287
  48.7 5.8 %collective-permute-start.4 = (bf16[2,80,1536]{2,1,0:T(8,128)(2,1)S(1)}, bf16[2,80,1536]{2,1,0:T(8,128)(2,1)}, u32[]{:S(2)}, u32[]{:S(2)}) collective-permute-start(bf16[2,80,1536]{2,1,0:T(8,128)(2,1)S(1)} %collective-permute-done.2.prev_ref), channel_id=1, source_target_pairs={{0,1},{1,0},{2,3},{3,2},{4,5},{5,4},{6,7},{7,6},{8,9},{9,8},{10,11... | collective-permute-start | bytes 1474568 | tf_op jit(solution)/shard_map/ppermute | solution.py:287
  51.7 3.9 %collective-permute-start.5 = (bf16[2,80,1536]{2,1,0:T(8,128)(2,1)S(1)}, bf16[2,80,1536]{2,1,0:T(8,128)(2,1)}, u32[]{:S(2)}, u32[]{:S(2)}) collective-permute-start(bf16[2,80,1536]{2,1,0:T(8,128)(2,1)S(1)} %collective-permute-done.3.next_ref), channel_id=1, source_target_pairs={{0,1},{1,0},{2,3},{3,2},{4,5},{5,4},{6,7},{7,6},{8,9},{9,8},{10,11... | collective-permute-start | bytes 1474568 | tf_op jit(solution)/shard_map/ppermute | solution.py:287
  59.6 1.2 copy-start.1
  60.9 1.0 copy-start.2
  61.9 1.0 copy-start.3
  62.9 0.7 copy-start.4
  63.6 0.7 copy-start.5
  78.8 1.3 copy-start
  80.1 11.1 %collective-permute-start.10 = (bf16[2,80,1536]{2,1,0:T(8,128)(2,1)S(1)}, bf16[2,80,1536]{2,1,0:T(8,128)(2,1)S(1)}, u32[]{:S(2)}, u32[]{:S(2)}) collective-permute-start(bf16[2,80,1536]{2,1,0:T(8,128)(2,1)S(1)} %get-tuple-element.28), channel_id=1, source_target_pairs={{0,1},{1,0},{2,3},{3,2},{4,5},{5,4},{6,7},{7,6},{8,9},{9,8},{10,11... | collective-permute-start | bytes 1474568 | tf_op jit(solution)/shard_map/ppermute | solution.py:287
  82.0 16.6 %collective-permute-start.12 = (bf16[2,80,1536]{2,1,0:T(8,128)(2,1)S(1)}, bf16[2,80,1536]{2,1,0:T(8,128)(2,1)S(1)}, u32[]{:S(2)}, u32[]{:S(2)}) collective-permute-start(bf16[2,80,1536]{2,1,0:T(8,128)(2,1)S(1)} %get-tuple-element.30), channel_id=1, source_target_pairs={{0,1},{1,0},{2,3},{3,2},{4,5},{5,4},{6,7},{7,6},{8,9},{9,8},{10,11... | collective-permute-start | bytes 1474568 | tf_op jit(solution)/shard_map/ppermute | solution.py:287
  84.4 41.8 %collective-permute-start.14 = (bf16[2,80,1536]{2,1,0:T(8,128)(2,1)S(1)}, bf16[2,80,1536]{2,1,0:T(8,128)(2,1)S(1)}, u32[]{:S(2)}, u32[]{:S(2)}) collective-permute-start(bf16[2,80,1536]{2,1,0:T(8,128)(2,1)S(1)} %get-tuple-element.31), channel_id=1, source_target_pairs={{1,66},{2,65},{3,68},{4,67},{5,70},{6,69},{7,72},{8,71},{9,74},{10... | collective-permute-start | bytes 1474568 | tf_op jit(solution)/shard_map/ppermute | solution.py:287
  88.0 95.4 %collective-permute-start.15 = (bf16[2,80,1536]{2,1,0:T(8,128)(2,1)}, bf16[2,80,1536]{2,1,0:T(8,128)(2,1)S(1)}, u32[]{:S(2)}, u32[]{:S(2)}) collective-permute-start(bf16[2,80,1536]{2,1,0:T(8,128)(2,1)} %get-tuple-element.32), channel_id=1, source_target_pairs={{65,2},{66,1},{67,4},{68,3},{69,6},{70,5},{71,8},{72,7},{73,10},{7... | collective-permute-start | bytes 1474568 | tf_op jit(solution)/shard_map/ppermute | solution.py:287
  89.3 94.1 %collective-permute-start.8 = (bf16[2,2,80,1536]{3,2,1,0:T(8,128)(2,1)}, bf16[2,2,80,1536]{3,2,1,0:T(8,128)(2,1)S(1)}, u32[]{:S(2)}, u32[]{:S(2)}) collective-permute-start(bf16[2,2,80,1536]{3,2,1,0:T(8,128)(2,1)} %get-tuple-element.25), channel_id=1, source_target_pairs={{0,1},{1,0},{2,3},{3,2},{4,5},{5,4},{6,7},{7,6},{8,9},{9,8},{10,11... | collective-permute-start | bytes 2949128 | tf_op jit(solution)/shard_map/ppermute | solution.py:287
  91.2 92.2 %collective-permute-start.9 = (bf16[2,2,80,1536]{3,2,1,0:T(8,128)(2,1)}, bf16[2,2,80,1536]{3,2,1,0:T(8,128)(2,1)S(1)}, u32[]{:S(2)}, u32[]{:S(2)}) collective-permute-start(bf16[2,2,80,1536]{3,2,1,0:T(8,128)(2,1)} %get-tuple-element.26), channel_id=1, source_target_pairs={{1,2},{2,1},{3,4},{4,3},{5,6},{6,5},{7,8},{8,7},{9,10},{10,9},{11,... | collective-permute-start | bytes 2949128 | tf_op jit(solution)/shard_map/ppermute | solution.py:287
  98.6 84.8 %collective-permute-start.11 = (bf16[2,80,1536]{2,1,0:T(8,128)(2,1)}, bf16[2,80,1536]{2,1,0:T(8,128)(2,1)}, u32[]{:S(2)}, u32[]{:S(2)}) collective-permute-start(bf16[2,80,1536]{2,1,0:T(8,128)(2,1)} %add_convert_fusion.1), channel_id=1, source_target_pairs={{0,64},{1,65},{2,66},{3,67},{4,68},{5,69},{6,70},{7,71},{8,72},{9,... | collective-permute-start | bytes 1474568 | tf_op jit(solution)/shard_map/ppermute | solution.py:287
  126.2 57.3 %copy-start.8 = (bf16[2,80,1536]{2,1,0:T(8,128)(2,1)}, bf16[2,80,1536]{2,1,0:T(8,128)(2,1)S(1)}, u32[]{:S(2)}) copy-start(bf16[2,80,1536]{2,1,0:T(8,128)(2,1)S(1)} %collective-permute-done.14.off_first_ref) | copy-start | bytes 1474564
  126.2 57.2 %collective-permute-start.13 = (bf16[2,80,1536]{2,1,0:T(8,128)(2,1)}, bf16[2,80,1536]{2,1,0:T(8,128)(2,1)}, u32[]{:S(2)}, u32[]{:S(2)}) collective-permute-start(bf16[2,80,1536]{2,1,0:T(8,128)(2,1)} %add_convert_fusion), channel_id=1, source_target_pairs={{64,0},{65,1},{66,2},{67,3},{68,4},{69,5},{70,6},{71,7},{72,8},{73... | collective-permute-start | bytes 1474568 | tf_op jit(solution)/shard_map/ppermute | solution.py:287
  183.4 0.8 copy-start.9
  183.4 1.1 copy-start.6
  183.5 1.4 copy-start.7

commit v2 on v1

v2 whole, which is shorter than its diff:
```python
import functools

import jax
import jax.numpy as jnp
from jax import lax
from jax.experimental import pallas as pl
from jax.experimental.pallas import tpu as pltpu
from jax.sharding import PartitionSpec as P

TILE_W = 8
EPSILON = 1e-06
HEAD_DIM = 128
LOG2E = 1.4426950408889634
BLOCKED = 1000.0
LANES = 128
BOTH = ("tm", "height")
SIZES = [(6, 6, 4), (7, 7, 5), (8, 8, 6)]
VMEM_BYTES = 56 * 1024 * 1024


def rms_inverse(full_rows):
    return lax.rsqrt(jnp.mean(full_rows * full_rows, axis=-1, keepdims=True) + EPSILON)


def norm_backward(grad_rows, unit_rows, inverse, gain_row):
    scaled = grad_rows * gain_row
    return inverse * (scaled - unit_rows * jnp.mean(unit_rows * scaled, axis=-1, keepdims=True))


def whole(memory_space=pltpu.VMEM):
    return pl.BlockSpec(memory_space=memory_space)


def params():
    return pltpu.CompilerParams(vmem_limit_bytes=VMEM_BYTES)


def head_lanes(g):
    return pl.ds(pl.multiple_of(g * LANES, LANES), LANES)


def pack_kernel(
    window_ref, key_ref, value_ref, gain_ref,
    slots_ref, own_ref, row_ref, first_ref, last_ref, corner_first_ref, corner_last_ref,
):
    frames, width, channels = key_ref.shape
    gain_row = gain_ref[...]
    edges = ((first_ref, corner_first_ref), (last_ref, corner_last_ref))

    def one_head(g, counts):
        lanes = head_lanes(g)
        row_on, frame_on = window_ref[g, 1], window_ref[g, 0]
        counts = tuple(c + on for c, on in zip(counts, (row_on, frame_on, row_on * frame_on)))
        slots = [jnp.maximum(c - 1, 0) for c in counts]
        for kind in range(3):
            slots_ref[kind, g] = slots[kind]
        pairs = []
        for f in range(frames):
            full_rows = key_ref[f, :, lanes].astype(jnp.float32)
            pairs.append(
                ((full_rows * rms_inverse(full_rows) * gain_row).astype(jnp.bfloat16), value_ref[f, :, lanes])
            )
            for c in range(2):
                own_ref[f, c, :, lanes] = pairs[f][c]

        @pl.when(row_on == 1)
        def _():
            for f in range(frames):
                for c in range(2):
                    row_ref[slots[0], f, c] = pairs[f][c]

        @pl.when(frame_on == 1)
        def _():
            for f in range(frames):
                for c in range(2):
                    edges[f][0][slots[1], c] = pairs[f][c]

        @pl.when(row_on * frame_on == 1)
        def _():
            for f in range(frames):
                for c in range(2):
                    edges[f][1][slots[2], c] = pairs[f][c]

        return counts

    zero = jnp.int32(0)
    lax.fori_loop(0, channels // LANES, one_head, (zero, zero, zero))


def pack(window, key_raw, values, key_gain, sizes):
    frames, width, channels = key_raw.shape
    kinds = jax.ShapeDtypeStruct
    low = jnp.bfloat16
    shapes = [(frames, 2, width, channels), (sizes[0], frames, 2, width, LANES)]
    shapes += [(sizes[1], 2, width, LANES)] * 2 + [(sizes[2], 2, width, LANES)] * 2
    return pl.pallas_call(
        pack_kernel,
        in_specs=[whole(pltpu.SMEM)] + [whole()] * 3,
        out_specs=[whole(pltpu.SMEM)] + [whole()] * 6,
        out_shape=[kinds((3, channels // LANES), jnp.int32)] + [kinds(shape, low) for shape in shapes],
        compiler_params=params(),
        name="pack_keys_values",
    )(window, key_raw, values, key_gain)


def matmul(a, b, dims):
    return lax.dot_general(a, b, (dims, ((), ())), preferred_element_type=jnp.float32)


def attend_kernel(
    window_ref, slots_ref, query_ref, grad_ref, own_ref, chip_ref, off_ref,
    prev_ref, next_ref, chip_prev_ref, chip_next_ref, off_prev_ref, off_next_ref,
    q_gain_ref, k_gain_ref,
    query_grad_ref, own_out, chip_out, off_out, prev_out, next_out, gain_out,
    key_buf, value_buf, key_sum, value_sum, gap_ref,
):
    frames, width, _ = query_ref.shape
    head_dim = LANES
    scale = head_dim ** (-0.5)

    key_buf[...] = jnp.zeros_like(key_buf)
    value_buf[...] = jnp.zeros_like(value_buf)
    gain_out[...] = jnp.zeros_like(gain_out)
    q_ids = lax.broadcasted_iota(jnp.int32, gap_ref.shape, 0)
    k_ids = lax.broadcasted_iota(jnp.int32, gap_ref.shape, 1)
    gap_ref[...] = jnp.abs(q_ids // TILE_W - k_ids % width // TILE_W).astype(jnp.float32)
    gain_row = q_gain_ref[...]
    full, part = span_sizes(width)
    t, h = lax.axis_index("tm"), lax.axis_index("height")
    has_off = jnp.logical_and(h > 0, h < lax.axis_size("height") - 1).astype(jnp.int32)
    has_prev = (t > 0).astype(jnp.int32)
    has_next = (t < lax.axis_size("tm") - 1).astype(jnp.int32)

    def one_head(g, carry):
        frame_reach = window_ref[g, 0]
        row_reach = window_ref[g, 1]
        tile_reach = window_ref[g, 2].astype(jnp.float32)
        row_count = 1 + 2 * row_reach
        lanes = head_lanes(g)
        row_slot, frame_slot, corner_slot = slots_ref[0, g], slots_ref[1, g], slots_ref[2, g]

        def place(r, e):
            return pl.ds(pl.multiple_of((e * row_count + r) * width, 16), width)

        def load(r, e, ref):
            key_buf[place(r, e)] = ref[0]
            value_buf[place(r, e)] = ref[1]

        def store(r, e, ref):
            ref[0] = key_sum[place(r, e)].astype(ref.dtype)
            ref[1] = value_sum[place(r, e)].astype(ref.dtype)

        def each_block(do, own, prev, following, chip, off, corners):
            for f in range(frames):
                do(0, f + 1, own[f])

            @pl.when(frame_reach == 1)
            def _():
                do(0, 0, prev)
                do(0, frames + 1, following)

            @pl.when(row_reach == 1)
            def _():
                for f in range(frames):
                    do(1, f + 1, chip[f])
                    do(2, f + 1, off[f])

            @pl.when(frame_reach * row_reach == 1)
            def _():
                for r in range(2):
                    do(r + 1, 0, corners[r][0])
                    do(r + 1, frames + 1, corners[r][1])

        each_block(
            load, [own_ref.at[f, :, :, lanes] for f in range(frames)], prev_ref.at[frame_slot], next_ref.at[frame_slot],
            [chip_ref.at[row_slot, f] for f in range(frames)], [off_ref.at[row_slot, f] for f in range(frames)],
            (
                (chip_prev_ref.at[frame_slot], chip_next_ref.at[frame_slot]),
                (off_prev_ref.at[corner_slot], off_next_ref.at[corner_slot]),
            ),
        )
        key_sum[...] = jnp.zeros_like(key_sum)
        value_sum[...] = jnp.zeros_like(value_sum)

        def work(keys):
            both = range(frames)
            k_block = lax.broadcasted_iota(jnp.int32, (1, keys), 1) // width
            frame = k_block // row_count
            row = k_block - frame * row_count
            gap = gap_ref[:, 0:keys]
            spans, unit, inverse, queries, grads, scores, prob_back, inside = [], [], [], [], [], [], [], []
            for f in both:
                start = (f + 1 - frame_reach) * row_count * width
                spans.append(pl.ds(pl.multiple_of(start, 16), keys))
                ext = f + 1 - frame_reach + frame
                shut = frame > 2 * frame_reach
                shut = jnp.logical_or(shut, jnp.logical_and(row == 2, has_off == 0))
                shut = jnp.logical_or(shut, jnp.logical_and(ext == 0, has_prev == 0))
                shut = jnp.logical_or(shut, jnp.logical_and(ext == frames + 1, has_next == 0))
                inside.append(gap + jnp.where(shut, BLOCKED, 0.0) <= tile_reach)
                full_rows = query_ref[f, :, lanes].astype(jnp.float32)
                inverse.append(rms_inverse(full_rows))
                unit.append(full_rows * inverse[f])
                queries.append((unit[f] * gain_row).astype(jnp.bfloat16))
                grads.append(grad_ref[f, :, lanes])
            for f in both:
                scores.append(matmul(queries[f], key_buf[spans[f]], ((1,), (1,))))
                prob_back.append(matmul(grads[f], value_buf[spans[f]], ((1,), (1,))))
            weight = [jnp.where(inside[f], jnp.exp2(scores[f] * (scale * LOG2E)), 0.0) for f in both]
            total = [jnp.sum(w, axis=-1, keepdims=True) for w in weight]
            inner = [jnp.sum(weight[f] * prob_back[f], axis=-1, keepdims=True) for f in both]
            over = [1.0 / x for x in total]
            prob = [weight[f] * over[f] for f in both]
            delta = [inner[f] * over[f] for f in both]
            score_back = [(prob[f] * ((prob_back[f] - delta[f]) * scale)).astype(jnp.bfloat16) for f in both]
            low = [p.astype(jnp.bfloat16) for p in prob]
            query_back = [matmul(score_back[f], key_buf[spans[f]], ((1,), (0,))) for f in both]
            key_back = [matmul(score_back[f], queries[f], ((0,), (0,))) for f in both]
            value_back = [matmul(low[f], grads[f], ((0,), (0,))) for f in both]
            for f in both:
                key_sum[spans[f]] += key_back[f]
                value_sum[spans[f]] += value_back[f]
                result = norm_backward(query_back[f], unit[f], inverse[f], gain_row)
                query_grad_ref[f, :, lanes] = result.astype(query_grad_ref.dtype)
            first = sum(jnp.sum(query_back[f] * unit[f], axis=0, keepdims=True) for f in both)
            second = sum(jnp.sum(query_back[f] * queries[f].astype(jnp.float32), axis=0, keepdims=True) for f in both)
            gain_out[0:1] += first
            gain_out[1:2] += second / k_gain_ref[...]

        wide = frame_reach * row_reach == 1
        pl.when(wide)(lambda: work(full))
        pl.when(jnp.logical_not(wide))(lambda: work(part))

        each_block(
            store, [own_out.at[g, f] for f in range(frames)], prev_out.at[frame_slot], next_out.at[frame_slot],
            [chip_out.at[row_slot, f + 1] for f in range(frames)], [off_out.at[row_slot, f + 1] for f in range(frames)],
            tuple((out.at[row_slot, 0], out.at[row_slot, frames + 1]) for out in (chip_out, off_out)),
        )
        return carry

    lax.fori_loop(0, window_ref.shape[0], one_head, 0)


def span_sizes(width):
    return tuple(-(-blocks * width // LANES) * LANES for blocks in (9, 3))


def attend(window, slots, query_raw, out_grad, own, chip, off, edges, corners, query_gain, key_gain):
    frames, width, channels = query_raw.shape
    heads = channels // LANES
    kinds = jax.ShapeDtypeStruct
    sent_shape = (chip.shape[0], frames + 2, 2, width, LANES)
    edge_shape = edges[0].shape
    most = 3 * width + span_sizes(width)[0]
    return pl.pallas_call(
        attend_kernel,
        in_specs=[whole(pltpu.SMEM)] * 2 + [whole()] * 13,
        out_specs=[whole()] * 7,
        out_shape=[
            kinds(query_raw.shape, jnp.bfloat16),
            kinds((heads, frames, 2, width, LANES), jnp.float32),
            kinds(sent_shape, jnp.bfloat16),
            kinds(sent_shape, jnp.bfloat16),
            kinds(edge_shape, jnp.float32),
            kinds(edge_shape, jnp.float32),
            kinds((2, LANES), jnp.float32),
        ],
        scratch_shapes=[
            pltpu.VMEM((most, LANES), jnp.bfloat16),
            pltpu.VMEM((most, LANES), jnp.bfloat16),
            pltpu.VMEM((most, LANES), jnp.float32),
            pltpu.VMEM((most, LANES), jnp.float32),
            pltpu.VMEM((width, span_sizes(width)[0]), jnp.float32),
        ],
        compiler_params=params(),
        name="attend",
    )(window, slots, query_raw, out_grad, own, chip, off, *edges, *corners, query_gain, key_gain)


def relay_kernel(window_ref, slots_ref, prev_ref, next_ref, chip_ref, off_ref, prev_out, next_out):
    last = chip_ref.shape[1] - 1

    def one_head(g, carry):
        row_on, frame_on = window_ref[g, 1], window_ref[g, 0]
        row_slot, frame_slot = slots_ref[0, g], slots_ref[1, g]

        @pl.when(jnp.logical_and(frame_on == 1, row_on == 0))
        def _():
            for kept, out in ((prev_ref, prev_out), (next_ref, next_out)):
                out[frame_slot] = kept[frame_slot].astype(out.dtype)

        @pl.when(jnp.logical_and(frame_on == 1, row_on == 1))
        def _():
            for kept, out, e in ((prev_ref, prev_out, 0), (next_ref, next_out, last)):
                terms = kept[frame_slot] + chip_ref[row_slot, e].astype(jnp.float32)
                out[frame_slot] = (terms + off_ref[row_slot, e].astype(jnp.float32)).astype(out.dtype)

        return carry

    lax.fori_loop(0, window_ref.shape[0], one_head, 0)


def relay(window, slots, kept, chip, off):
    return pl.pallas_call(
        relay_kernel,
        in_specs=[whole(pltpu.SMEM)] * 2 + [whole()] * 4,
        out_specs=[whole()] * 2,
        out_shape=[jax.ShapeDtypeStruct(kept[0].shape, jnp.bfloat16)] * 2,
        compiler_params=params(),
        name="add_corner_terms",
    )(window, slots, *kept, chip, off)


def finish_kernel(
    window_ref, slots_ref, key_ref, own_ref, chip_ref, off_ref, first_ref, last_ref, gain_ref,
    key_grad_ref, value_grad_ref,
):
    frames = key_ref.shape[0]
    gain_row = gain_ref[...]
    edges = (first_ref, last_ref)

    def one_head(g, carry):
        lanes = head_lanes(g)
        row_on, frame_on = window_ref[g, 1] == 1, window_ref[g, 0] == 1
        row_slot, frame_slot = slots_ref[0, g], slots_ref[1, g]
        for f in range(frames):
            sums = []
            for c in range(2):
                rows = chip_ref[row_slot, f + 1, c].astype(jnp.float32) + off_ref[row_slot, f + 1, c].astype(jnp.float32)
                edge = edges[f][frame_slot, c].astype(jnp.float32)
                sums.append(own_ref[g, f, c] + jnp.where(row_on, rows, 0.0) + jnp.where(frame_on, edge, 0.0))
            full_rows = key_ref[f, :, lanes].astype(jnp.float32)
            inverse = rms_inverse(full_rows)
            result = norm_backward(sums[0], full_rows * inverse, inverse, gain_row)
            key_grad_ref[f, :, lanes] = result.astype(key_grad_ref.dtype)
            value_grad_ref[f, :, lanes] = sums[1].astype(value_grad_ref.dtype)
        return carry

    lax.fori_loop(0, window_ref.shape[0], one_head, 0, unroll=2)


def finish(window, slots, key_raw, own, chip, off, edges, key_gain):
    frames, width, _ = key_raw.shape
    return pl.pallas_call(
        finish_kernel,
        in_specs=[whole(pltpu.SMEM)] * 2 + [whole()] * 7,
        out_specs=[whole()] * 2,
        out_shape=[jax.ShapeDtypeStruct(key_raw.shape, jnp.bfloat16)] * 2,
        compiler_params=params(),
        name="finish_keys",
    )(window, slots, key_raw, own, chip, off, *edges, key_gain)


def off_chip(h):
    return h + 1 if h % 2 else h - 1


def move(block, frame_step, row_rule):
    frames_size, rows_size = lax.axis_size("tm"), lax.axis_size("height")
    route = []
    for t in range(frames_size):
        for h in range(rows_size):
            to_t, to_h = t + frame_step, row_rule(h)
            if 0 <= to_t < frames_size and 0 <= to_h < rows_size:
                route.append((t * rows_size + h, to_t * rows_size + to_h))
    return lax.ppermute(block, BOTH, route)


def same_row(h):
    return h


def chip_row(h):
    return h ^ 1


def sum_over_rows(part):
    rows_size = lax.axis_size("height")
    per_row = LANES // rows_size
    pieces = part.reshape(2, rows_size, per_row).transpose(1, 0, 2).reshape(rows_size, 2 * per_row)
    return lax.all_to_all(pieces, "height", 0, 0, tiled=True).sum(0, keepdims=True)


def sum_over_frames(mine):
    copies = jnp.broadcast_to(mine, (lax.axis_size("tm"), mine.shape[1]))
    return lax.all_to_all(copies, "tm", 0, 0, tiled=True).sum(0).reshape(2, mine.shape[1] // 2)


def with_sizes(sizes, query_flat, key_flat, value_flat, grad_flat, q_gain, k_gain, window):
    slots, own, rows, first, last, corner_first, corner_last = pack(window, key_flat, value_flat, k_gain, sizes)
    off = move(rows, 0, off_chip)
    prev = move(last, 1, same_row)
    following = move(first, -1, same_row)
    off_prev = move(corner_last, 1, off_chip)
    off_next = move(corner_first, -1, off_chip)
    rows, prev, following, off_prev, off_next = lax.optimization_barrier((rows, prev, following, off_prev, off_next))
    chip = move(rows, 0, chip_row)
    chip_prev = move(prev, 0, chip_row)
    chip_next = move(following, 0, chip_row)

    query_grad, own_sum, chip_sum, off_sum, prev_sum, next_sum, gain_part = attend(
        window, slots, query_flat, grad_flat, own, chip, off,
        (prev, following, chip_prev, chip_next), (off_prev, off_next), q_gain, k_gain,
    )

    off_back = move(off_sum, 0, off_chip)
    chip_back = move(chip_sum, 0, chip_row)
    mine = sum_over_rows(gain_part)
    chip_back, off_back, mine = lax.optimization_barrier((chip_back, off_back, mine))
    prev_all, next_all = relay(window, slots, (prev_sum, next_sum), chip_back, off_back)
    last_back = move(prev_all, -1, same_row)
    first_back = move(next_all, 1, same_row)
    gain_grad = sum_over_frames(mine)
    first_back, last_back, gain_grad = lax.optimization_barrier((first_back, last_back, gain_grad))
    key_grad, value_grad = finish(
        window, slots, key_flat, own_sum, chip_back, off_back, (first_back, last_back), k_gain
    )
    return query_grad, key_grad, value_grad, gain_grad


def on_device(query_raw, key_raw, values, out_grad, query_gain, key_gain, window):
    frames, _, width, channels = query_raw.shape
    heads = channels // LANES
    flat = (frames, width, channels)
    row_on, frame_on = window[:, 1], window[:, 0]
    row_count, frame_count, both_count = jnp.sum(row_on), jnp.sum(frame_on), jnp.sum(row_on * frame_on)
    choices = SIZES + [(heads, heads, heads)]
    choice = jnp.int32(0)
    for sizes in SIZES:
        fits = (row_count <= sizes[0]) & (frame_count <= sizes[1]) & (both_count <= sizes[2])
        choice += 1 - fits.astype(jnp.int32)
    args = [x.reshape(flat) for x in (query_raw, key_raw, values, out_grad)]
    outs = lax.switch(
        choice,
        [functools.partial(with_sizes, sizes) for sizes in choices],
        *args, query_gain[None], key_gain[None], window,
    )
    return tuple(x.reshape(query_raw.shape) for x in outs[:3]) + (outs[3],)


def solution(mesh):
    token = P("tm", "height", None, None)
    return jax.shard_map(
        on_device,
        mesh=mesh,
        in_specs=(token, token, token, token, P(), P(), P()),
        out_specs=(token, token, token, P(None, "height")),
        check_vma=False,
    )
```

time: 195 us -> 141 us (0.72)
  the two profiles are of different devices: /device:TPU:1 before, /device:TPU:5 now
where the time goes in v2:
time: 141 us; the launch traced here: 140 us
  starting transfers between devices  48.6 us (34%)
  blocking collectives  42.6 us (30%)
  Pallas kernels  27.2 us (19%)
  waiting for transfers between devices  6.77 us (5%)
  between operations  6.48 us (5%)
  local copies, waits for them, and re-layouts  6.32 us (4%)
  other arithmetic  1.54 us (1%)
    ppermute x12, starting transfers between devices, move(): return lax.ppermute(block, BOTH, route)  48.6 us
    all_to_all x1, blocking collectives, sum_over_rows(): lax.all_to_all(pieces, 'height', 0, 0, tiled=True).sum(0, keepdims=True)  30.9 us
    pallas_call x1, Pallas kernels, attend(): pl.pallas_call(attend_kernel, in_specs=[whole(pltpu.SMEM)] * 2 + [whole()...  15.4 us
    all_to_all x1, blocking collectives, sum_over_frames(): lax.all_to_all(copies, 'tm', 0, 0, tiled=True).sum(0)  11.7 us
    ppermute x12, waiting for transfers between devices, move(): return lax.ppermute(block, BOTH, route)  6.77 us
    pallas_call x1, Pallas kernels, finish(): pl.pallas_call(finish_kernel, in_specs=[whole(pltpu.SMEM)] * 2 + [whole()...  4.54 us
    pallas_call x1, Pallas kernels, pack(): pl.pallas_call(pack_kernel, in_specs=[whole(pltpu.SMEM)] + [whole()] * 3,...  4.15 us
    cond x28, local copies, waits for them, and re-layouts  3.32 us
  transfers between devices with their start and end apart: 12, of which 3 were waited for; matrix products, arithmetic and copies ran while one was open for 1% of the time, Pallas kernels for 0%

profile of v2, /device:TPU:5, one launch (start us, length us, event | category | flops | bytes accessed | tf_op | source)
XLA Modules:
  0.0 139.9 jit_solution(7148563214661939403)
XLA Ops:
  0.6 1.4 %multiply_reduce_fusion = (s32[]{:T(128)}, s32[]{:T(128)}, s32[]{:T(128)}) fusion(s32[12,3]{0,1:T(4,128)} %param.17), kind=kLoop, calls=%fused_computation | loop fusion | flops 45 | bytes 108 | tf_op jit(solution)/shard_map/reduce_sum | solution.py:426
  7.9 131.4 %conditional.1 = (bf16[2,80,1536]{2,1,0:T(8,128)(2,1)}, bf16[2,80,1536]{2,1,0:T(8,128)(2,1)}, bf16[2,80,1536]{2,1,0:T(8,128)(2,1)}, f32[2,2]{1,0:T(2,128)S(1)}) conditional(s32[]{:T(128)} %clamp.3, (s32[12,3]{0,1:T(4,128)}, bf16[2,80,1536]{2,1,0:T(8,128)(2,1)}, bf16[2,80,1536]{2,1,0:T(8,128)(2,1)}, ...), branch_computations={%region_3.0_spmd, %region_6.0_spmd, %region_9.0_spmd, %region_12.0... | conditional | flops 280 | bytes 72757984 | solution.py:433
  7.9 1.4 copy.60.window_ref
  9.3 4.2 %pack_keys_values.5 = (s32[3,12]{1,0:T(4,128)}, bf16[2,2,80,1536]{3,2,1,0:T(8,128)(2,1)}, bf16[7,2,2,80,128]{4,3,2,1,0:T(8,128)(2,1)}, bf16[7,2,80,128]{3,2,1,0:...) custom-call(s32[12,3]{1,0:T(8,128)} %copy.60.window_ref, ...), custom_call_target="tpu_custom_call" | custom-call | tf_op jit(solution)/shard_map/cond/branch_1_fun/pack_keys_values/pallas_call | solution.py:96
  13.4 3.2 %collective-permute-start.12 = (bf16[7,2,80,128]{3,2,1,0:T(8,128)(2,1)}, bf16[7,2,80,128]{3,2,1,0:T(8,128)(2,1)S(1)}, u32[]{:S(2)}, u32[]{:S(2)}) collective-permute-start(bf16[7,2,80,128]{3,2,1,0:T(8,128)(2,1)} %get-tuple-element.101), channel_id=1, source_target_pairs={{0,64},{1,65},{2,66},{3,67},{4,68},{5,69},{6,70},{7,71},{8,72},{9,... | collective-permute-start | bytes 860168 | tf_op jit(solution)/shard_map/cond/branch_1_fun/ppermute | solution.py:366
  16.7 3.0 %collective-permute-start.13 = (bf16[7,2,80,128]{3,2,1,0:T(8,128)(2,1)}, bf16[7,2,80,128]{3,2,1,0:T(8,128)(2,1)S(1)}, u32[]{:S(2)}, u32[]{:S(2)}) collective-permute-start(bf16[7,2,80,128]{3,2,1,0:T(8,128)(2,1)} %get-tuple-element.102), channel_id=1, source_target_pairs={{64,0},{65,1},{66,2},{67,3},{68,4},{69,5},{70,6},{71,7},{72,8},{73... | collective-permute-start | bytes 860168 | tf_op jit(solution)/shard_map/cond/branch_1_fun/ppermute | solution.py:366
  19.6 4.9 %collective-permute-start.14 = (bf16[5,2,80,128]{3,2,1,0:T(8,128)(2,1)}, bf16[5,2,80,128]{3,2,1,0:T(8,128)(2,1)S(1)}, u32[]{:S(2)}, u32[]{:S(2)}) collective-permute-start(bf16[5,2,80,128]{3,2,1,0:T(8,128)(2,1)} %get-tuple-element.103), channel_id=1, source_target_pairs={{1,66},{2,65},{3,68},{4,67},{5,70},{6,69},{7,72},{8,71},{9,74},{10... | collective-permute-start | bytes 614408 | tf_op jit(solution)/shard_map/cond/branch_1_fun/ppermute | solution.py:366
  24.5 2.8 %collective-permute-start.15 = (bf16[5,2,80,128]{3,2,1,0:T(8,128)(2,1)}, bf16[5,2,80,128]{3,2,1,0:T(8,128)(2,1)S(1)}, u32[]{:S(2)}, u32[]{:S(2)}) collective-permute-start(bf16[5,2,80,128]{3,2,1,0:T(8,128)(2,1)} %get-tuple-element.104), channel_id=1, source_target_pairs={{65,2},{66,1},{67,4},{68,3},{69,6},{70,5},{71,8},{72,7},{73,10},{7... | collective-permute-start | bytes 614408 | tf_op jit(solution)/shard_map/cond/branch_1_fun/ppermute | solution.py:366
  27.3 4.7 %collective-permute-start.17 = (bf16[7,2,2,80,128]{4,3,2,1,0:T(8,128)(2,1)}, bf16[7,2,2,80,128]{4,3,2,1,0:T(8,128)(2,1)S(1)}, u32[]{:S(2)}, u32[]{:S(2)}) collective-permute-start(bf16[7,2,2,80,128]{4,3,2,1,0:T(8,128)(2,1)} %get-tuple-element.105), channel_id=1, source_target_pairs={{1,2},{2,1},{3,4},{4,3},{5,6},{6,5},{7,8},{8,7},{9,10},{10,9},{11,... | collective-permute-start | bytes 1720328 | tf_op jit(solution)/shard_map/cond/branch_1_fun/ppermute | solution.py:366
  32.1 0.9 collective-permute-done.15.off_next_ref
  33.0 1.9 %collective-permute-start.16 = (bf16[7,2,2,80,128]{4,3,2,1,0:T(8,128)(2,1)}, bf16[7,2,2,80,128]{4,3,2,1,0:T(8,128)(2,1)S(1)}, u32[]{:S(2)}, u32[]{:S(2)}) collective-permute-start(bf16[7,2,2,80,128]{4,3,2,1,0:T(8,128)(2,1)} %get-tuple-element.105), channel_id=1, source_target_pairs={{0,1},{1,0},{2,3},{3,2},{4,5},{5,4},{6,7},{7,6},{8,9},{9,8},{10,11... | collective-permute-start | bytes 1720328 | tf_op jit(solution)/shard_map/cond/branch_1_fun/ppermute | solution.py:366
  35.0 2.4 %collective-permute-start.18 = (bf16[7,2,80,128]{3,2,1,0:T(8,128)(2,1)S(1)}, bf16[7,2,80,128]{3,2,1,0:T(8,128)(2,1)S(1)}, u32[]{:S(2)}, u32[]{:S(2)}) collective-permute-start(bf16[7,2,80,128]{3,2,1,0:T(8,128)(2,1)S(1)} %collective-permute-done.12.prev_ref), channel_id=1, source_target_pairs={{0,1},{1,0},{2,3},{3,2},{4,5},{5,4},{6,7},{7,6},{8,9},{9,8},{10,11... | collective-permute-start | bytes 860168 | tf_op jit(solution)/shard_map/cond/branch_1_fun/ppermute | solution.py:366
  37.4 1.9 %collective-permute-start.19 = (bf16[7,2,80,128]{3,2,1,0:T(8,128)(2,1)S(1)}, bf16[7,2,80,128]{3,2,1,0:T(8,128)(2,1)S(1)}, u32[]{:S(2)}, u32[]{:S(2)}) collective-permute-start(bf16[7,2,80,128]{3,2,1,0:T(8,128)(2,1)S(1)} %collective-permute-done.13.next_ref), channel_id=1, source_target_pairs={{0,1},{1,0},{2,3},{3,2},{4,5},{5,4},{6,7},{7,6},{8,9},{9,8},{10,11... | collective-permute-start | bytes 860168 | tf_op jit(solution)/shard_map/cond/branch_1_fun/ppermute | solution.py:366
  39.3 1.5 %collective-permute-done.19.chip_next_ref = bf16[7,2,80,128]{3,2,1,0:T(8,128)(2,1)S(1)} collective-permute-done((bf16[7,2,80,128]{3,2,1,0:T(8,128)(2,1)S(1)}, bf16[7,2,80,128]{3,2,1,0:T(8,128)(2,1)S(1)}, u32[]{:S(2)}, u32[]{:S(2)}) %collective-permute-start.19) | collective-permute-done | bytes 286752 | tf_op jit(solution)/shard_map/cond/branch_1_fun/ppermute | solution.py:366
  40.9 4.3 %collective-permute-done.17.off_ref = bf16[7,2,2,80,128]{4,3,2,1,0:T(8,128)(2,1)S(1)} collective-permute-done((bf16[7,2,2,80,128]{4,3,2,1,0:T(8,128)(2,1)}, bf16[7,2,2,80,128]{4,3,2,1,0:T(8,128)(2,1)S(1)}, u32[]{:S(2)}, u32[]{:S(2)}) %collective-permute-start.17) | collective-permute-done | bytes 573472 | tf_op jit(solution)/shard_map/cond/branch_1_fun/ppermute | solution.py:366
  45.2 0.8 copy-done.15
  46.0 0.3 copy-done.16
  46.3 15.4 %attend.5 = (bf16[2,80,1536]{2,1,0:T(8,128)(2,1)}, f32[12,2,2,80,128]{4,3,2,1,0:T(8,128)}, bf16[7,4,2,80,128]{4,3,2,1,0:T(8,128)(2,1)}, bf16[7,4,2,80,128]{4,3,2...) custom-call(s32[12,3]{1,0:T(8,128)} %copy.60.window_ref, ...), custom_call_target="tpu_custom_call" | custom-call | tf_op jit(solution)/shard_map/cond/branch_1_fun/attend/pallas_call | solution.py:255
  61.7 2.1 %collective-permute-start.20 = (bf16[7,4,2,80,128]{4,3,2,1,0:T(8,128)(2,1)}, bf16[7,4,2,80,128]{4,3,2,1,0:T(8,128)(2,1)S(1)}, u32[]{:S(2)}, u32[]{:S(2)}) collective-permute-start(bf16[7,4,2,80,128]{4,3,2,1,0:T(8,128)(2,1)} %get-tuple-element.113), channel_id=1, source_target_pairs={{0,1},{1,0},{2,3},{3,2},{4,5},{5,4},{6,7},{7,6},{8,9},{9,8},{10,11... | collective-permute-start | bytes 3440648 | tf_op jit(solution)/shard_map/cond/branch_1_fun/ppermute | solution.py:366
  63.8 15.5 %collective-permute-start.21 = (bf16[7,4,2,80,128]{4,3,2,1,0:T(8,128)(2,1)}, bf16[7,4,2,80,128]{4,3,2,1,0:T(8,128)(2,1)S(1)}, u32[]{:S(2)}, u32[]{:S(2)}) collective-permute-start(bf16[7,4,2,80,128]{4,3,2,1,0:T(8,128)(2,1)} %get-tuple-element.114), channel_id=1, source_target_pairs={{1,2},{2,1},{3,4},{4,3},{5,6},{6,5},{7,8},{8,7},{9,10},{10,9},{11,... | collective-permute-start | bytes 3440648 | tf_op jit(solution)/shard_map/cond/branch_1_fun/ppermute | solution.py:366
  79.3 0.8 reshape.81
  80.4 30.9 %all_to_all.50 = f32[64,1,4]{2,1,0:T(1,128)S(1)} all-to-all(f32[64,1,4]{2,1,0:T(1,128)S(1)} %copy.51), channel_id=1, replica_groups=mesh['tm'=8,'height'=64] {'height'}, dimensions={0} | all-to-all | bytes 2048 | tf_op jit(solution)/shard_map/cond/branch_1_fun/all_to_all | solution.py:381
  111.4 1.0 copy-done.7
  112.4 0.4 copy-done.8
  112.8 3.1 %add_corner_terms.5 = (bf16[7,2,80,128]{3,2,1,0:T(8,128)(2,1)}, bf16[7,2,80,128]{3,2,1,0:T(8,128)(2,1)}) custom-call(s32[12,3]{1,0:T(8,128)} %copy.60.window_ref, s32[3,12]{1,0:T(4,128)} %get-tuple-element.96.slots_ref, f32[7,2,80,128]{3,2,1,0:T(8,128)} %get-tuple-element.118.prev_ref, f32[7,2,80,128]{3,2,1,0:T(8,128)} %get-tuple-element.119.next_ref, ...), custom_call_target="tpu_custom_call" | custom-call | tf_op jit(solution)/shard_map/cond/branch_1_fun/add_corner_terms/pallas_call | solution.py:304
  115.9 2.0 %collective-permute-start.22 = (bf16[7,2,80,128]{3,2,1,0:T(8,128)(2,1)}, bf16[7,2,80,128]{3,2,1,0:T(8,128)(2,1)S(1)}, u32[]{:S(2)}, u32[]{:S(2)}) collective-permute-start(bf16[7,2,80,128]{3,2,1,0:T(8,128)(2,1)} %get-tuple-element.120), channel_id=1, source_target_pairs={{0,64},{1,65},{2,66},{3,67},{4,68},{5,69},{6,70},{7,71},{8,72},{9,... | collective-permute-start | bytes 860168 | tf_op jit(solution)/shard_map/cond/branch_1_fun/ppermute | solution.py:366
  117.9 4.2 %collective-permute-start.23 = (bf16[7,2,80,128]{3,2,1,0:T(8,128)(2,1)}, bf16[7,2,80,128]{3,2,1,0:T(8,128)(2,1)S(1)}, u32[]{:S(2)}, u32[]{:S(2)}) collective-permute-start(bf16[7,2,80,128]{3,2,1,0:T(8,128)(2,1)} %get-tuple-element.121), channel_id=1, source_target_pairs={{64,0},{65,1},{66,2},{67,3},{68,4},{69,5},{70,6},{71,7},{72,8},{73... | collective-permute-start | bytes 860168 | tf_op jit(solution)/shard_map/cond/branch_1_fun/ppermute | solution.py:366
  122.1 11.7 %all_to_all.51 = f32[8,1,4]{2,1,0:T(1,128)S(1)} all-to-all(f32[8,1,4]{2,1,0:T(1,128)S(1)} %broadcast_in_dim.21), channel_id=1, replica_groups=mesh['tm'=8,'height'=64] {'tm'}, dimensions={0} | all-to-all | bytes 256 | tf_op jit(solution)/shard_map/cond/branch_1_fun/all_to_all | solution.py:386
  133.9 0.7 copy-done.37
  134.6 0.1 copy-done.38
  134.8 4.5 %finish_keys.5 = (bf16[2,80,1536]{2,1,0:T(8,128)(2,1)}, bf16[2,80,1536]{2,1,0:T(8,128)(2,1)}) custom-call(s32[12,3]{1,0:T(8,128)} %copy.60.window_ref, s32[3,12]{1,0:T(4,128)} %get-tuple-element.96.slots_ref, bf16[2,80,1536]{2,1,0:T(8,128)(2,1)S(1)} %copy-done.1, f32[12,2,2,80,128]{4,3,2,1,0:T(8,128)} %get-tuple-element.112.own_ref, ...), custom_call_target="tpu_custom_call" | custom-call | tf_op jit(solution)/shard_map/cond/branch_1_fun/finish_keys/pallas_call | solution.py:344
  139.3 0.6 copy-done.55
  (38 shorter events, 0.5 us)
Async XLA Ops:
  13.4 19.6 %collective-permute-start.12 = (bf16[7,2,80,128]{3,2,1,0:T(8,128)(2,1)}, bf16[7,2,80,128]{3,2,1,0:T(8,128)(2,1)S(1)}, u32[]{:S(2)}, u32[]{:S(2)}) collective-permute-start(bf16[7,2,80,128]{3,2,1,0:T(8,128)(2,1)} %get-tuple-element.101), channel_id=1, source_target_pairs={{0,64},{1,65},{2,66},{3,67},{4,68},{5,69},{6,70},{7,71},{8,72},{9,... | collective-permute-start | bytes 860168 | tf_op jit(solution)/shard_map/cond/branch_1_fun/ppermute | solution.py:366
  16.7 16.4 %collective-permute-start.13 = (bf16[7,2,80,128]{3,2,1,0:T(8,128)(2,1)}, bf16[7,2,80,128]{3,2,1,0:T(8,128)(2,1)S(1)}, u32[]{:S(2)}, u32[]{:S(2)}) collective-permute-start(bf16[7,2,80,128]{3,2,1,0:T(8,128)(2,1)} %get-tuple-element.102), channel_id=1, source_target_pairs={{64,0},{65,1},{66,2},{67,3},{68,4},{69,5},{70,6},{71,7},{72,8},{73... | collective-permute-start | bytes 860168 | tf_op jit(solution)/shard_map/cond/branch_1_fun/ppermute | solution.py:366
  19.6 12.4 %collective-permute-start.14 = (bf16[5,2,80,128]{3,2,1,0:T(8,128)(2,1)}, bf16[5,2,80,128]{3,2,1,0:T(8,128)(2,1)S(1)}, u32[]{:S(2)}, u32[]{:S(2)}) collective-permute-start(bf16[5,2,80,128]{3,2,1,0:T(8,128)(2,1)} %get-tuple-element.103), channel_id=1, source_target_pairs={{1,66},{2,65},{3,68},{4,67},{5,70},{6,69},{7,72},{8,71},{9,74},{10... | collective-permute-start | bytes 614408 | tf_op jit(solution)/shard_map/cond/branch_1_fun/ppermute | solution.py:366
  24.5 8.5 %collective-permute-start.15 = (bf16[5,2,80,128]{3,2,1,0:T(8,128)(2,1)}, bf16[5,2,80,128]{3,2,1,0:T(8,128)(2,1)S(1)}, u32[]{:S(2)}, u32[]{:S(2)}) collective-permute-start(bf16[5,2,80,128]{3,2,1,0:T(8,128)(2,1)} %get-tuple-element.104), channel_id=1, source_target_pairs={{65,2},{66,1},{67,4},{68,3},{69,6},{70,5},{71,8},{72,7},{73,10},{7... | collective-permute-start | bytes 614408 | tf_op jit(solution)/shard_map/cond/branch_1_fun/ppermute | solution.py:366
  27.3 17.8 %collective-permute-start.17 = (bf16[7,2,2,80,128]{4,3,2,1,0:T(8,128)(2,1)}, bf16[7,2,2,80,128]{4,3,2,1,0:T(8,128)(2,1)S(1)}, u32[]{:S(2)}, u32[]{:S(2)}) collective-permute-start(bf16[7,2,2,80,128]{4,3,2,1,0:T(8,128)(2,1)} %get-tuple-element.105), channel_id=1, source_target_pairs={{1,2},{2,1},{3,4},{4,3},{5,6},{6,5},{7,8},{8,7},{9,10},{10,9},{11,... | collective-permute-start | bytes 1720328 | tf_op jit(solution)/shard_map/cond/branch_1_fun/ppermute | solution.py:366
  32.1 13.1 %copy-start.47 = (bf16[5,2,80,128]{3,2,1,0:T(8,128)(2,1)}, bf16[5,2,80,128]{3,2,1,0:T(8,128)(2,1)S(1)}, u32[]{:S(2)}) copy-start(bf16[5,2,80,128]{3,2,1,0:T(8,128)(2,1)S(1)} %collective-permute-done.14.off_prev_ref) | copy-start | bytes 614404 | tf_op jit(solution)/shard_map/cond
  33.0 12.2 %copy-start.48 = (bf16[5,2,80,128]{3,2,1,0:T(8,128)(2,1)}, bf16[5,2,80,128]{3,2,1,0:T(8,128)(2,1)S(1)}, u32[]{:S(2)}) copy-start(bf16[5,2,80,128]{3,2,1,0:T(8,128)(2,1)S(1)} %collective-permute-done.15.off_next_ref) | copy-start | bytes 614404 | tf_op jit(solution)/shard_map/cond
  33.0 12.2 %copy-start.33 = (bf16[7,2,80,128]{3,2,1,0:T(8,128)(2,1)}, bf16[7,2,80,128]{3,2,1,0:T(8,128)(2,1)S(1)}, u32[]{:S(2)}) copy-start(bf16[7,2,80,128]{3,2,1,0:T(8,128)(2,1)S(1)} %collective-permute-done.12.prev_ref) | copy-start | bytes 860164 | tf_op jit(solution)/shard_map/cond
  33.0 12.2 %copy-start.34 = (bf16[7,2,80,128]{3,2,1,0:T(8,128)(2,1)}, bf16[7,2,80,128]{3,2,1,0:T(8,128)(2,1)S(1)}, u32[]{:S(2)}) copy-start(bf16[7,2,80,128]{3,2,1,0:T(8,128)(2,1)S(1)} %collective-permute-done.13.next_ref) | copy-start | bytes 860164 | tf_op jit(solution)/shard_map/cond
  33.0 12.1 %collective-permute-start.16 = (bf16[7,2,2,80,128]{4,3,2,1,0:T(8,128)(2,1)}, bf16[7,2,2,80,128]{4,3,2,1,0:T(8,128)(2,1)S(1)}, u32[]{:S(2)}, u32[]{:S(2)}) collective-permute-start(bf16[7,2,2,80,128]{4,3,2,1,0:T(8,128)(2,1)} %get-tuple-element.105), channel_id=1, source_target_pairs={{0,1},{1,0},{2,3},{3,2},{4,5},{5,4},{6,7},{7,6},{8,9},{9,8},{10,11... | collective-permute-start | bytes 1720328 | tf_op jit(solution)/shard_map/cond/branch_1_fun/ppermute | solution.py:366
  35.0 4.3 %collective-permute-start.18 = (bf16[7,2,80,128]{3,2,1,0:T(8,128)(2,1)S(1)}, bf16[7,2,80,128]{3,2,1,0:T(8,128)(2,1)S(1)}, u32[]{:S(2)}, u32[]{:S(2)}) collective-permute-start(bf16[7,2,80,128]{3,2,1,0:T(8,128)(2,1)S(1)} %collective-permute-done.12.prev_ref), channel_id=1, source_target_pairs={{0,1},{1,0},{2,3},{3,2},{4,5},{5,4},{6,7},{7,6},{8,9},{9,8},{10,11... | collective-permute-start | bytes 860168 | tf_op jit(solution)/shard_map/cond/branch_1_fun/ppermute | solution.py:366
  37.4 3.5 %collective-permute-start.19 = (bf16[7,2,80,128]{3,2,1,0:T(8,128)(2,1)S(1)}, bf16[7,2,80,128]{3,2,1,0:T(8,128)(2,1)S(1)}, u32[]{:S(2)}, u32[]{:S(2)}) collective-permute-start(bf16[7,2,80,128]{3,2,1,0:T(8,128)(2,1)S(1)} %collective-permute-done.13.next_ref), channel_id=1, source_target_pairs={{0,1},{1,0},{2,3},{3,2},{4,5},{5,4},{6,7},{7,6},{8,9},{9,8},{10,11... | collective-permute-start | bytes 860168 | tf_op jit(solution)/shard_map/cond/branch_1_fun/ppermute | solution.py:366
  39.3 5.9 %copy-start.35 = (bf16[7,2,80,128]{3,2,1,0:T(8,128)(2,1)}, bf16[7,2,80,128]{3,2,1,0:T(8,128)(2,1)S(1)}, u32[]{:S(2)}) copy-start(bf16[7,2,80,128]{3,2,1,0:T(8,128)(2,1)S(1)} %collective-permute-done.18.chip_prev_ref) | copy-start | bytes 860164 | tf_op jit(solution)/shard_map/cond
  40.8 4.4 %copy-start.36 = (bf16[7,2,80,128]{3,2,1,0:T(8,128)(2,1)}, bf16[7,2,80,128]{3,2,1,0:T(8,128)(2,1)S(1)}, u32[]{:S(2)}) copy-start(bf16[7,2,80,128]{3,2,1,0:T(8,128)(2,1)S(1)} %collective-permute-done.19.chip_next_ref) | copy-start | bytes 860164 | tf_op jit(solution)/shard_map/cond
  45.2 0.9 copy-start.15
  45.2 1.1 copy-start.16
  61.7 73.0 %copy-start.1 = (bf16[2,80,1536]{2,1,0:T(8,128)(2,1)S(1)}, bf16[2,80,1536]{2,1,0:T(8,128)(2,1)}, u32[]{:S(2)}) copy-start(bf16[2,80,1536]{2,1,0:T(8,128)(2,1)} %get-tuple-element.93.key_ref) | copy-start | bytes 1474564 | tf_op jit(solution)/shard_map/cond
  61.7 73.0 %copy-start.52 = (f32[1,128]{1,0:T(1,128)S(1)}, f32[1,128]{1,0:T(1,128)}, u32[]{:S(2)}) copy-start(f32[1,128]{1,0:T(1,128)} %get-tuple-element.95.gain_ref.k_gain_ref) | copy-start | bytes 1540 | tf_op jit(solution)/shard_map/cond
  61.7 49.6 %collective-permute-start.20 = (bf16[7,4,2,80,128]{4,3,2,1,0:T(8,128)(2,1)}, bf16[7,4,2,80,128]{4,3,2,1,0:T(8,128)(2,1)S(1)}, u32[]{:S(2)}, u32[]{:S(2)}) collective-permute-start(bf16[7,4,2,80,128]{4,3,2,1,0:T(8,128)(2,1)} %get-tuple-element.113), channel_id=1, source_target_pairs={{0,1},{1,0},{2,3},{3,2},{4,5},{5,4},{6,7},{7,6},{8,9},{9,8},{10,11... | collective-permute-start | bytes 3440648 | tf_op jit(solution)/shard_map/cond/branch_1_fun/ppermute | solution.py:366
  63.8 47.5 %collective-permute-start.21 = (bf16[7,4,2,80,128]{4,3,2,1,0:T(8,128)(2,1)}, bf16[7,4,2,80,128]{4,3,2,1,0:T(8,128)(2,1)S(1)}, u32[]{:S(2)}, u32[]{:S(2)}) collective-permute-start(bf16[7,4,2,80,128]{4,3,2,1,0:T(8,128)(2,1)} %get-tuple-element.114), channel_id=1, source_target_pairs={{1,2},{2,1},{3,4},{4,3},{5,6},{6,5},{7,8},{8,7},{9,10},{10,9},{11,... | collective-permute-start | bytes 3440648 | tf_op jit(solution)/shard_map/cond/branch_1_fun/ppermute | solution.py:366
  111.3 1.1 copy-start.7
  111.4 1.4 %copy-start.8 = (bf16[7,4,2,80,128]{4,3,2,1,0:T(8,128)(2,1)}, bf16[7,4,2,80,128]{4,3,2,1,0:T(8,128)(2,1)S(1)}, u32[]{:S(2)}) copy-start(bf16[7,4,2,80,128]{4,3,2,1,0:T(8,128)(2,1)S(1)} %collective-permute-done.21.off_ref) | copy-start | bytes 3440644 | tf_op jit(solution)/shard_map/cond
  115.9 18.0 %collective-permute-start.22 = (bf16[7,2,80,128]{3,2,1,0:T(8,128)(2,1)}, bf16[7,2,80,128]{3,2,1,0:T(8,128)(2,1)S(1)}, u32[]{:S(2)}, u32[]{:S(2)}) collective-permute-start(bf16[7,2,80,128]{3,2,1,0:T(8,128)(2,1)} %get-tuple-element.120), channel_id=1, source_target_pairs={{0,64},{1,65},{2,66},{3,67},{4,68},{5,69},{6,70},{7,71},{8,72},{9,... | collective-permute-start | bytes 860168 | tf_op jit(solution)/shard_map/cond/branch_1_fun/ppermute | solution.py:366
  117.9 16.1 %collective-permute-start.23 = (bf16[7,2,80,128]{3,2,1,0:T(8,128)(2,1)}, bf16[7,2,80,128]{3,2,1,0:T(8,128)(2,1)S(1)}, u32[]{:S(2)}, u32[]{:S(2)}) collective-permute-start(bf16[7,2,80,128]{3,2,1,0:T(8,128)(2,1)} %get-tuple-element.121), channel_id=1, source_target_pairs={{64,0},{65,1},{66,2},{67,3},{68,4},{69,5},{70,6},{71,7},{72,8},{73... | collective-permute-start | bytes 860168 | tf_op jit(solution)/shard_map/cond/branch_1_fun/ppermute | solution.py:366
  133.9 0.7 copy-start.37
  133.9 0.8 copy-start.38
  139.3 0.6 copy-start.55
